TPU v7x, 256 devices: a whole 4x4x8 slice. The times are simulated.
256 devices in a mesh: ctx: 32 (over z_lo, x, y), exp: 8 (over z_hi, core).
Axes of the slice: x: 4, y: 4, z: 8 (z_hi: 4, z_lo: 2; z = z_hi * 2 + z_lo), core: 2. Of those that a mesh axis runs over, the one named last changes fastest.
Arguments:
- query: bfloat16 [4096, 2048], P('ctx', 'exp'), may hold values from -5 to 5
- keys: bfloat16 [4096, 2048], P('ctx', 'exp'), may hold values from -5 to 5
- values: bfloat16 [4096, 2048], P('ctx', 'exp'), may hold values from -5 to 5
- resid: bfloat16 [4096, 4096], P('ctx'), may hold values from -6 to 6
- flags: int32 [4096], P('ctx'), may hold values from 0 to 1, as said below
- routes: int32 [4096, 6], P('ctx'), may hold values from 0 to 63, all different within a row; in each aligned block of 16 rows (0 to 15, 16 to 31, ...) at most 2 rows name the same one
- gates: bfloat16 [4096, 6], P('ctx'), may hold values from 0.049804688 to 0.3984375
- out_weight: bfloat16 [2048, 4096], P('exp'), may hold values from -0.125 to 0.125
- norm_gain: float32 [4096], replicated, may hold values from 0.1 to 1.9
- img_gate: bfloat16 [4096, 5504], P('exp', 'ctx'), may hold values from -0.09375 to 0.09375
- img_up: bfloat16 [4096, 5504], P('exp', 'ctx'), may hold values from -0.09375 to 0.09375
- img_down: bfloat16 [4096, 5504], P('exp', 'ctx'), may hold values from -0.078125 to 0.078125
- exp_gate: bfloat16 [256, 4096, 352], P(('ctx', 'exp')), may hold values from -0.09375 to 0.09375
- exp_up: bfloat16 [256, 4096, 352], P(('ctx', 'exp')), may hold values from -0.09375 to 0.09375
- exp_down: bfloat16 [256, 352, 4096], P(('ctx', 'exp')), may hold values from -0.15625 to 0.15625
Outputs:
- layer_out: bfloat16 [4096, 4096], P(('ctx', 'exp'))
Inputs may be any that keep to these rules, and one draw needn't show every extreme that they name: `routes`: in each aligned block of 16 rows, no expert is named by more than 2 rows. `flags`: in each aligned block of 16 positions at most 8 are image positions; some block holds exactly 8.
All inputs are finite; a program needn't handle non-finite values.
Results may differ from a plain program's by a relative error of at most 0.02.
Values may be sent and summed in bfloat16 or wider, within the bound.
A program may use at most 128 MiB of HBM per device.

v0:
```python
import math

import jax
import jax.numpy as jnp
from jax import lax
from jax.sharding import PartitionSpec as P

HEAD_DIM = 128
EXPERTS = 64
TOP = 6
CAP = 2


NEGATIVE = -1e30
EPSILON = 1e-05


def root_norm(hidden_state, norm_gain):
    power = jnp.mean(hidden_state * hidden_state, axis=-1, keepdims=True)
    return (hidden_state * lax.rsqrt(power + EPSILON) * norm_gain).astype(jnp.bfloat16)


def slot_ranks(route_ids, text_rows):
    blocks, row_count, top_count = route_ids.shape
    flat = route_ids.reshape(blocks, row_count * top_count)
    usable = jnp.broadcast_to(text_rows[:, :, None], (blocks, row_count, top_count)).reshape(
        blocks, row_count * top_count
    )
    onehot = (flat[:, :, None] == jnp.arange(EXPERTS, dtype=jnp.int32)[None, None, :]) & usable[
        :, :, None
    ]
    counts = jnp.cumsum(onehot.astype(jnp.int32), axis=1)
    slot_rank = jnp.sum(jnp.where(onehot, counts, 0), axis=2) - 1
    return (
        slot_rank.reshape(blocks, row_count, top_count),
        usable.reshape(blocks, row_count, top_count),
    )


def expert_apply(batch, exp_gate, exp_up, exp_down):
    gate_part = jnp.einsum("clmd,ldf->clmf", batch, exp_gate, preferred_element_type=jnp.float32)
    up_part = jnp.einsum("clmd,ldf->clmf", batch, exp_up, preferred_element_type=jnp.float32)
    active = (jax.nn.silu(gate_part) * up_part).astype(jnp.bfloat16)
    return jnp.einsum(
        "clmf,lfd->clmd", active, exp_down, preferred_element_type=jnp.float32
    ).astype(jnp.bfloat16)


def body(
    query,
    keys,
    values,
    resid,
    flags,
    routes,
    gates,
    out_weight,
    norm_gain,
    img_gate,
    img_up,
    img_down,
    exp_gate,
    exp_up,
    exp_down,
):
    context_count = lax.axis_size("ctx")
    expert_count = lax.axis_size("exp")
    context_index = lax.axis_index("ctx")
    expert_index = lax.axis_index("exp")
    ctx_rows = query.shape[0]
    row_count = ctx_rows // expert_count
    model_width = resid.shape[1]
    local_heads = query.shape[1] // HEAD_DIM
    score_scale = 1.0 / math.sqrt(HEAD_DIM)
    query_spot = context_index * ctx_rows + jnp.arange(ctx_rows, dtype=jnp.int32)
    query_heads = query.reshape(ctx_rows, local_heads, HEAD_DIM)
    running_max = jnp.full((local_heads, ctx_rows), NEGATIVE, jnp.float32)
    key_part = lax.all_gather(keys, "ctx", axis=0, tiled=True)
    value_part = lax.all_gather(values, "ctx", axis=0, tiled=True)
    amount = key_part.shape[0]
    key_heads = key_part.reshape(amount, local_heads, HEAD_DIM)
    value_heads = value_part.reshape(amount, local_heads, HEAD_DIM)
    scores = (
        jnp.einsum("qhd,khd->hqk", query_heads, key_heads, preferred_element_type=jnp.float32)
        * score_scale
    )
    allowed = jnp.arange(amount, dtype=jnp.int32)[None, :] <= query_spot[:, None]
    scores = jnp.where(allowed[None], scores, NEGATIVE)
    new_max = jnp.maximum(running_max, jnp.max(scores, axis=-1))
    weights = jnp.where(allowed[None], jnp.exp(scores - new_max[..., None]), 0.0)
    running_sum = jnp.sum(weights, axis=-1)
    running_out = jnp.einsum(
        "hqk,khd->hqd",
        weights.astype(jnp.bfloat16),
        value_heads,
        preferred_element_type=jnp.float32,
    )
    running_max, running_sum, running_out = (new_max, running_sum, running_out)
    attended = (
        (running_out / running_sum[..., None])
        .transpose(1, 0, 2)
        .reshape(ctx_rows, local_heads * HEAD_DIM)
        .astype(jnp.bfloat16)
    )
    own_start = expert_index * row_count
    head_total = lax.psum(
        jnp.dot(attended, out_weight, preferred_element_type=jnp.float32).astype(jnp.bfloat16),
        "exp",
    ).astype(jnp.float32)
    hidden_state = resid.astype(jnp.float32) + head_total
    normed = root_norm(hidden_state, norm_gain)
    state_own = lax.dynamic_slice_in_dim(hidden_state, own_start, row_count, 0)
    normed_own = lax.dynamic_slice_in_dim(normed, own_start, row_count, 0)
    image_gate, image_up, image_down = (
        lax.all_gather(img_gate, "exp", axis=0, tiled=True),
        lax.all_gather(img_up, "exp", axis=0, tiled=True),
        lax.all_gather(img_down, "exp", axis=0, tiled=True),
    )
    own_flags = lax.dynamic_slice_in_dim(flags, own_start, row_count, 0)
    portion = lax.all_gather(normed_own, "ctx", axis=0, tiled=True)
    gate_part = jnp.dot(portion, image_gate, preferred_element_type=jnp.float32)
    up_part = jnp.dot(portion, image_up, preferred_element_type=jnp.float32)
    image_act = (jax.nn.silu(gate_part) * up_part).astype(jnp.bfloat16)
    portion = image_act
    image_out = lax.psum_scatter(
        lax.dot_general(
            portion, image_down, (((1,), (1,)), ((), ())), preferred_element_type=jnp.float32
        ).astype(jnp.bfloat16),
        "ctx",
        scatter_dimension=0,
        tiled=True,
    ).astype(jnp.float32)
    split_count = max(1, context_count * expert_count // EXPERTS)
    group_count = EXPERTS // context_count
    local_count = exp_gate.shape[0]
    first_local = expert_index // split_count * local_count
    text_rows = flags == 0
    slot_rank, usable = slot_ranks(
        routes.reshape(expert_count, row_count, TOP), text_rows.reshape(expert_count, row_count)
    )
    slot_rank = slot_rank.reshape(ctx_rows, TOP)
    usable = usable.reshape(ctx_rows, TOP)
    subset = jnp.arange(ctx_rows, dtype=jnp.int32)[:, None] // row_count
    target = routes // group_count
    local_id = routes % group_count - first_local
    valid = usable & (local_id >= 0) & (local_id < local_count)
    slot_id = jnp.where(
        valid, ((target * local_count + local_id) * expert_count + subset) * CAP + slot_rank, -1
    )
    slot_total = context_count * local_count * expert_count * CAP
    matches = slot_id[None] == jnp.arange(slot_total, dtype=jnp.int32)[:, None, None]
    dispatch = jnp.any(matches, axis=-1).astype(jnp.bfloat16)
    weighting = jnp.sum(jnp.where(matches, gates[None].astype(jnp.float32), 0.0), axis=-1).astype(
        jnp.bfloat16
    )
    outgoing = jnp.dot(dispatch, normed, preferred_element_type=jnp.float32).astype(jnp.bfloat16)
    outgoing = outgoing.reshape(context_count, local_count, expert_count * CAP, model_width)
    returned = lax.all_to_all(
        expert_apply(
            lax.all_to_all(outgoing, "ctx", split_axis=0, concat_axis=0, tiled=True),
            exp_gate,
            exp_up,
            exp_down,
        ),
        "ctx",
        split_axis=0,
        concat_axis=0,
        tiled=True,
    )
    returned_flat = returned.reshape(slot_total, model_width)
    portion = weighting
    text_out = lax.psum_scatter(
        lax.dot_general(
            portion, returned_flat, (((0,), (0,)), ((), ())), preferred_element_type=jnp.float32
        ).astype(jnp.bfloat16),
        "exp",
        scatter_dimension=0,
        tiled=True,
    ).astype(jnp.float32)
    layer_out = state_own + jnp.where(own_flags[:, None] == 1, image_out, text_out)
    return layer_out.astype(jnp.bfloat16)


def solution(mesh):
    return jax.shard_map(
        body,
        mesh=mesh,
        in_specs=(
            P("ctx", "exp"),
            P("ctx", "exp"),
            P("ctx", "exp"),
            P("ctx", None),
            P("ctx"),
            P("ctx", None),
            P("ctx", None),
            P("exp", None),
            P(),
            P("exp", "ctx"),
            P("exp", "ctx"),
            P("exp", "ctx"),
            P(("ctx", "exp"), None, None),
            P(("ctx", "exp"), None, None),
            P(("ctx", "exp"), None, None),
        ),
        out_specs=P(("ctx", "exp"), None),
        check_vma=False,
    )
```

profile of v0, /device:TPU:1, one launch (start us, length us, event | category | flops | bytes accessed | tf_op | source)
XLA Modules:
  0.0 923.5 jit_solution(13128138780802805475)
XLA Ops:
  9.5 115.2 %all-gather.7.cloned.1.call-done = bf16[4096,256]{0,1:T(8,128)(2,1)} async-done(((bf16[128,256]{0,1:T(8,128)(2,1)}), bf16[4096,256]{0,1:T(8,128)(2,1)}) %all-gather.7.cloned.1.call-update) | async-done | bytes 2097168 | tf_op jit(solution)/shard_map/all_gather | solution.py:78
  124.7 2.8 fusion.84
  127.5 1.9 copy-done.1
  130.5 146.3 %all-gather.9.cloned.1.call-done = bf16[4096,256]{1,0:T(8,128)(2,1)} async-done(((bf16[128,256]{1,0:T(8,128)(2,1)}), bf16[4096,256]{1,0:T(8,128)(2,1)}) %all-gather.9.cloned.1.call-update) | async-done | bytes 2097168 | tf_op jit(solution)/shard_map/all_gather | solution.py:79
  276.9 4.1 copy.66
  281.0 4.0 fusion.49
  287.1 96.0 %all-reduce.2.cloned.1.call-done = bf16[128,4096]{1,0:T(8,128)(2,1)} async-done(((bf16[128,4096]{1,0:T(8,128)(2,1)}), bf16[128,4096]{1,0:T(8,128)(2,1)}) %all-reduce.2.cloned.1.call-update) | async-done | bytes 1048592 | tf_op jit(solution)/shard_map/psum | solution.py:106
  383.1 3.4 convert_add_fusion
  389.3 2.1 select_reduce_fusion.1
  392.1 4.4 convolution_convert_fusion
  396.5 7.1 all-to-all-start
  404.9 65.5 %all-to-all-done = bf16[32,1,16,4096]{3,2,1,0:T(8,128)(2,1)} async-done(((bf16[32,1,16,4096]{3,2,1,0:T(8,128)(2,1)}), bf16[32,1,16,4096]{3,2,1,0:T(8,128)(2,1)}, u32[]{:S(2)}, u32[]{:S(2)}) %all-to-all-start) | async-done | bytes 4194336 | tf_op jit(solution)/shard_map/all_to_all | solution.py:160
  470.4 6.4 fusion.17
  476.7 9.8 %fusion = bf16[32,1,16,4096]{3,2,1,0:T(8,128)(2,1)} fusion(bf16[1,352,4096]{2,1,0:T(8,128)(2,1)S(1)} %copy-done, bf16[1,4096,352]{1,2,0:T(8,128)(2,1)} %param.28, bf16[32,1,16,4096]{3,2,1,0:T(8,128)(2,1)} %all-to-all-done, f32[32,1,16,352]{3,2,0,1:T(8,128)} %fusion.17), kind=kOutput, calls=%fused_computation.3 | convolution fusion | flops 2955968512 | bytes 14876672 | tf_op jit(solution)/shard_map/clmf,lfd->clmd/dot_general | solution.py:44
  486.5 9.5 %all-to-all-start.1 = ((bf16[32,1,16,4096]{3,2,1,0:T(8,128)(2,1)}), bf16[32,1,16,4096]{3,2,1,0:T(8,128)(2,1)}, u32[]{:S(2)}, u32[]{:S(2)}) async-start(bf16[32,1,16,4096]{3,2,1,0:T(8,128)(2,1)} %fusion), calls=%async_computation.2 | async-start | bytes 8388608 | tf_op jit(solution)/shard_map/all_to_all | solution.py:158
  496.1 119.4 %all-gather.11.cloned.1.call-done = bf16[512,4096]{1,0:T(8,128)(2,1)} async-done(((bf16[16,4096]{1,0:T(8,128)(2,1)}), bf16[512,4096]{1,0:T(8,128)(2,1)}) %all-gather.11.cloned.1.call-update) | async-done | bytes 4194320 | tf_op jit(solution)/shard_map/all_gather | solution.py:120
  615.5 4.2 fusion.85
  619.7 49.4 %all-gather.17.cloned.1.call-done = bf16[4096,172]{0,1:T(8,128)(2,1)} async-done(((bf16[512,172]{0,1:T(8,128)(2,1)}), bf16[4096,172]{0,1:T(8,128)(2,1)}) %all-gather.17.cloned.1.call-update) | async-done | bytes 1409040 | tf_op jit(solution)/shard_map/all_gather | solution.py:117
  669.0 32.5 %all-gather.15.cloned.1.call-done = bf16[4096,172]{0,1:T(8,128)(2,1)} async-done(((bf16[512,172]{0,1:T(8,128)(2,1)}), bf16[4096,172]{0,1:T(8,128)(2,1)}) %all-gather.15.cloned.1.call-update) | async-done | bytes 1409040 | tf_op jit(solution)/shard_map/all_gather | solution.py:116
  701.6 7.8 convolution_convert_fusion.1
  710.3 3.9 convolution_convert_fusion.3
  714.3 141.0 %reduce-scatter.3.cloned.1.call-done = bf16[16,4096]{1,0:T(8,128)(2,1)} async-done(((bf16[512,4096]{1,0:T(8,128)(2,1)}), bf16[16,4096]{1,0:T(8,128)(2,1)}) %reduce-scatter.3.cloned.1.call-update) | async-done | bytes 131088 | tf_op jit(solution)/shard_map/reduce_scatter | solution.py:125
  855.3 59.8 %reduce-scatter.5.cloned.1.call-done = bf16[16,4096]{1,0:T(8,128)(2,1)} async-done(((bf16[128,4096]{1,0:T(8,128)(2,1)}), bf16[16,4096]{1,0:T(8,128)(2,1)}) %reduce-scatter.5.cloned.1.call-update) | async-done | bytes 131088 | tf_op jit(solution)/shard_map/reduce_scatter | solution.py:172
  915.1 1.8 add_convert_fusion
  (66 shorter events, 11.7 us)
Async XLA Ops:
  6.5 470.2 %copy-start = (bf16[1,352,4096]{2,1,0:T(8,128)(2,1)S(1)}, bf16[1,352,4096]{2,1,0:T(8,128)(2,1)}, u32[]{:S(2)}) copy-start(bf16[1,352,4096]{2,1,0:T(8,128)(2,1)} %param.29) | copy-start | bytes 8650756
  6.5 118.1 %all-gather.7.cloned.1.call-start = ((), (), s32[]{:S(2)}) async-start(), calls=%async_computation.4 | async-start | bytes 2162688 | tf_op jit(solution)/shard_map/all_gather | solution.py:78
  8.3 268.6 %all-gather.9.cloned.1.call-start = ((), (), s32[]{:S(2)}) async-start(), calls=%async_computation.5 | async-start | bytes 2162688 | tf_op jit(solution)/shard_map/all_gather | solution.py:79
  9.0 374.0 %all-reduce.2.cloned.1.call-start = ((), (), s32[]{:S(2)}) async-start(), calls=%async_computation.6 | async-start | bytes 2097152 | tf_op jit(solution)/shard_map/psum | solution.py:106
  127.5 2.0 copy-start.1
  281.0 4.0 copy-start.5
  286.4 100.0 %copy-start.6 = (f32[4096]{0:T(1024)S(1)}, f32[4096]{0:T(1024)}, u32[]{:S(2)}) copy-start(f32[4096]{0:T(1024)} %param.23) | copy-start | bytes 49156
  286.5 209.6 %all-gather.13.cloned.1.call-start = ((), (), s32[]{:S(2)}) async-start(), calls=%async_computation.8 | async-start | bytes 1622016 | tf_op jit(solution)/shard_map/all_gather | solution.py:115
  287.0 328.4 %all-gather.11.cloned.1.call-start = ((), (), s32[]{:S(2)}) async-start(), calls=%async_computation.7 | async-start | bytes 4325376 | tf_op jit(solution)/shard_map/all_gather | solution.py:120
  287.1 101.5 %copy-start.7 = (s32[128,6]{0,1:T(8,128)S(1)}, s32[128,6]{0,1:T(8,128)}, u32[]{:S(2)}) copy-start(s32[128,6]{0,1:T(8,128)} %param.20) | copy-start | bytes 9220
  383.1 3.4 copy-start.3
  383.1 3.4 copy-start.4
  386.4 2.4 copy-start.9
  386.9 1.0 copy-start.2
  396.5 73.9 %all-to-all-start = ((bf16[32,1,16,4096]{3,2,1,0:T(8,128)(2,1)}), bf16[32,1,16,4096]{3,2,1,0:T(8,128)(2,1)}, u32[]{:S(2)}, u32[]{:S(2)}) async-start(bf16[32,1,16,4096]{3,2,1,0:T(8,128)(2,1)} %bitcast.109), calls=%async_computation.1 | async-start | bytes 8388608 | tf_op jit(solution)/shard_map/all_to_all | solution.py:160
  403.6 265.4 %all-gather.17.cloned.1.call-start = ((), (), s32[]{:S(2)}) async-start(), calls=%async_computation.10 | async-start | bytes 1622016 | tf_op jit(solution)/shard_map/all_gather | solution.py:117
  404.2 297.4 %all-gather.15.cloned.1.call-start = ((), (), s32[]{:S(2)}) async-start(), calls=%async_computation.9 | async-start | bytes 1622016 | tf_op jit(solution)/shard_map/all_gather | solution.py:116
  486.5 223.7 %all-to-all-start.1 = ((bf16[32,1,16,4096]{3,2,1,0:T(8,128)(2,1)}), bf16[32,1,16,4096]{3,2,1,0:T(8,128)(2,1)}, u32[]{:S(2)}, u32[]{:S(2)}) async-start(bf16[32,1,16,4096]{3,2,1,0:T(8,128)(2,1)} %fusion), calls=%async_computation.2 | async-start | bytes 8388608 | tf_op jit(solution)/shard_map/all_to_all | solution.py:158
  496.0 359.3 %reduce-scatter.3.cloned.1.call-start = ((), (), s32[]{:S(2)}) async-start(), calls=%async_computation.11 | async-start | bytes 4325376 | tf_op jit(solution)/shard_map/reduce_scatter | solution.py:125
  709.4 0.7 copy-start.8
  709.4 205.7 %reduce-scatter.5.cloned.1.call-start = ((), (), s32[]{:S(2)}) async-start(), calls=%async_computation.12 | async-start | bytes 1179648 | tf_op jit(solution)/shard_map/reduce_scatter | solution.py:172
Sparse Core Ops, SparseCore 0:
  9.1 115.5 all-gather.6
  126.4 150.3 all-gather.8
  286.6 96.4 all-reduce.1
  384.8 34.5 all-gather.12
  421.1 194.3 all-gather.10
  617.2 51.8 all-gather.16
  670.9 30.6 all-gather.14
  709.5 145.6 reduce-scatter.2
  857.8 57.2 reduce-scatter.4
where the time goes:
time: 925 us; the launch traced here: 923 us
  waiting for transfers between devices  827 us (89%)
  matrix products  44.7 us (5%)
  starting transfers between devices  17.1 us (2%)
  between operations  13.4 us (1%)
  local copies, waits for them, and re-layouts  10.9 us (1%)
  other arithmetic  9.79 us (1%)
    all_gather x1, waiting for transfers between devices, body(): value_part = lax.all_gather(values, 'ctx', axis=0, tiled=True)  146 us
    reduce_scatter x1, waiting for transfers between devices, body(): lax.psum_scatter(lax.dot_general(portion, image_down, (((1,), (1,)), ((),...  141 us
    all_gather x1, waiting for transfers between devices, body(): portion = lax.all_gather(normed_own, 'ctx', axis=0, tiled=True)  119 us
    all_gather x1, waiting for transfers between devices, body(): key_part = lax.all_gather(keys, 'ctx', axis=0, tiled=True)  115 us
    psum x1, waiting for transfers between devices, body(): lax.psum(jnp.dot(attended, out_weight, preferred_element_type=jnp.float32...  96 us
    all_to_all x1, waiting for transfers between devices, body(): lax.all_to_all(outgoing, 'ctx', split_axis=0, concat_axis=0, tiled=True)  65.5 us
    reduce_scatter x1, waiting for transfers between devices, body(): lax.psum_scatter(lax.dot_general(portion, returned_flat, (((0,), (0,)), (...  59.8 us
    all_gather x1, waiting for transfers between devices, body(): lax.all_gather(img_down, 'exp', axis=0, tiled=True)  49.4 us
  transfers between devices with their start and end apart: 11, of which 9 were waited for; matrix products, arithmetic and copies ran while one was open for 5% of the time, Pallas kernels for 0%

commit v1 on v0

--- a/solution.py
+++ b/solution.py
@@ -1,24 +1,218 @@
+import functools
 import math
 
 import jax
 import jax.numpy as jnp
 from jax import lax
+from jax.experimental import pallas as pl
+from jax.experimental.pallas import tpu as pltpu
 from jax.sharding import PartitionSpec as P
 
+MESH = pl.DeviceIdType.MESH
 HEAD_DIM = 128
+NEGATIVE = -1e30
+EPSILON = 1e-05
+WIDTH = 4096
+CHUNK = 1024
+CHUNKS = WIDTH // CHUNK
+
+
+class Place:
+    def __init__(self):
+        c, e = lax.axis_index("ctx"), lax.axis_index("exp")
+        self.c, self.e = c, e
+        self.zl, self.x, self.y = lax.div(c, 16), lax.rem(lax.div(c, 4), 4), lax.rem(c, 4)
+        self.zh, self.k = lax.div(e, 2), lax.rem(e, 2)
+        self.z = self.zh * 2 + self.zl
+
+    def dev(self, dx=0, dy=0, dzl=0, dzh=0, dk=0):
+        x, y = lax.rem(self.x + dx + 4, 4), lax.rem(self.y + dy + 4, 4)
+        zl, zh, k = lax.rem(self.zl + dzl, 2), lax.rem(self.zh + dzh + 4, 4), lax.rem(self.k + dk, 2)
+        return (zl * 16 + x * 4 + y, zh * 2 + k)
+
+
+def remote(src, dst, send, recv, device):
+    return pltpu.make_async_remote_copy(
+        src_ref=src, dst_ref=dst, send_sem=send, recv_sem=recv, device_id=device, device_id_type=MESH
+    )
+
+
+def attention_kernel(
+    q_ref, k_ref, v_ref, resid_ref, gain_ref, ow_ref,
+    state_ref, normed_ref,
+    kbuf, vbuf, qbuf, obuf, stat, rbuf, rstat, ow, res, att, pbuf, sbuf, tbuf, zbuf,
+    kv_send, kv_recv, q_send, q_recv, o_send, o_recv, s_send, s_recv, c_send, c_recv, z_send, z_recv, local_sem,
+):
+    at = Place()
+    load_w = pltpu.make_async_copy(ow_ref, ow, local_sem.at[0])
+    load_w.start()
+    load_r = pltpu.make_async_copy(resid_ref.at[pl.ds(pl.multiple_of(at.e * 16, 16), 16)], res, local_sem.at[1])
+    load_r.start()
+    barrier = pltpu.get_barrier_semaphore()
+    partners = [at.dev(dx=d) for d in (1, 2, 3)]
+    partners += [at.dev(dzl=j // 4, dy=j % 4) for j in range(1, 8)]
+    partners += [at.dev(dk=1)] + [at.dev(dzh=d) for d in (1, 2, 3)]
+    for device in partners:
+        pl.semaphore_signal(barrier, inc=1, device_id=device, device_id_type=MESH)
+    kbuf[0] = k_ref[...]
+    vbuf[0] = v_ref[...]
+    qbuf[0] = q_ref[...]
+    pl.semaphore_wait(barrier, len(partners))
+
+    kv = []
+    for d in (1, 2, 3):
+        kv.append(remote(k_ref, kbuf.at[d], kv_send.at[0, d], kv_recv.at[0, d], at.dev(dx=d)))
+        kv.append(remote(v_ref, vbuf.at[d], kv_send.at[1, d], kv_recv.at[1, d], at.dev(dx=d)))
+    qs = [None] + [
+        remote(q_ref, qbuf.at[j], q_send.at[j], q_recv.at[j], at.dev(dzl=j // 4, dy=j % 4)) for j in range(1, 8)
+    ]
+    for j in range(1, 8):
+        qs[j].start()
+    for copy in kv:
+        copy.start()
+
+    rows = lax.broadcasted_iota(jnp.int32, (512, 128), 0)
+    lanes = lax.broadcasted_iota(jnp.int32, (512, 128), 1)
+    from_x = lax.rem(at.x - lax.div(rows, 128) + 4, 4)
+    key_spot = (at.zl * 16 + from_x * 4 + at.y) * 128 + lax.rem(rows, 128) - lanes
+    for copy in kv:
+        copy.wait_recv()
+
+    def back(j):
+        device = at.dev(dzl=lax.div(j, 4), dy=4 - lax.rem(j, 4))
+        return (
+            remote(obuf.at[j], rbuf.at[j], o_send.at[j], o_recv.at[j], device),
+            remote(stat.at[j], rstat.at[j], s_send.at[j], s_recv.at[j], device),
+        )
+
+    def one_block(j, _):
+        @pl.when(j > 0)
+        def _():
+            remote(q_ref, qbuf.at[j], q_send.at[j], q_recv.at[j], at.dev(dzl=lax.div(j, 4), dy=lax.rem(j, 4))).wait_recv()
+
+        q_zl = lax.rem(at.zl + lax.div(j, 4), 2)
+        q_y = lax.rem(at.y + 4 - lax.rem(j, 4), 4)
+        limit = (q_zl * 16 + at.x * 4 + q_y) * 128
+        allowed = key_spot <= limit
+        stats = []
+        for h in range(2):
+            cols = slice(h * HEAD_DIM, (h + 1) * HEAD_DIM)
+            kh = kbuf[:, :, cols].reshape(512, HEAD_DIM)
+            vh = vbuf[:, :, cols].reshape(512, HEAD_DIM)
+            qh = qbuf[j, :, cols]
+            s = lax.dot_general(kh, qh, (((1,), (1,)), ((), ())), preferred_element_type=jnp.float32)
+            s = jnp.where(allowed, s * (1.0 / math.sqrt(HEAD_DIM)), NEGATIVE)
+            m = jnp.max(s, axis=0, keepdims=True)
+            p = jnp.where(allowed, jnp.exp(s - m), 0.0)
+            l = jnp.sum(p, axis=0, keepdims=True)
+            o = lax.dot_general(vh, p.astype(jnp.bfloat16), (((0,), (0,)), ((), ())), preferred_element_type=jnp.float32)
+            obuf[j, cols, :] = o.astype(jnp.bfloat16)
+            stats += [m, l]
+        stat[j] = jnp.concatenate(stats + stats, axis=0)
+
+        @pl.when(j > 0)
+        def _():
+            for copy in back(j):
+                copy.start()
+
+        return 0
+
+    lax.fori_loop(0, 8, one_block, 0)
+    rbuf[0] = obuf[0]
+    rstat[0] = stat[0]
+    for j in range(1, 8):
+        for copy in back(j):
+            copy.wait_recv()
+    for h in range(2):
+        cols = slice(h * HEAD_DIM, (h + 1) * HEAD_DIM)
+        top = rstat[0, 2 * h:2 * h + 1, :]
+        for j in range(1, 8):
+            top = jnp.maximum(top, rstat[j, 2 * h:2 * h + 1, :])
+        total = jnp.zeros((HEAD_DIM, 128), jnp.float32)
+        denom = jnp.zeros((1, 128), jnp.float32)
+        for j in range(8):
+            w = jnp.exp(rstat[j, 2 * h:2 * h + 1, :] - top)
+            denom += w * rstat[j, 2 * h + 1:2 * h + 2, :]
+            total += w * rbuf[j, cols, :].astype(jnp.float32)
+        att[cols, :] = (total / denom).astype(jnp.bfloat16)
+
+    load_w.wait()
+    load_r.wait()
+    swaps, sums = [], []
+    for n in range(CHUNKS):
+        cols = pl.ds(n * CHUNK, CHUNK)
+        part = lax.dot_general(
+            att[...], ow[:, cols], (((0,), (0,)), ((), ())), preferred_element_type=jnp.float32
+        ).astype(jnp.bfloat16)
+        for b in range(8):
+            pbuf[b % 2, b // 2, :, cols] = part[16 * b:16 * b + 16]
+        copy = remote(pbuf.at[1 - at.k, :, :, cols], sbuf.at[:, :, cols], c_send.at[n], c_recv.at[n], at.dev(dk=1))
+        copy.start()
+        swaps.append(copy)
+    for n in range(CHUNKS):
+        cols = pl.ds(n * CHUNK, CHUNK)
+        swaps[n].wait_recv()
+        tbuf[:, :, cols] = (
+            pbuf[at.k, :, :, cols].astype(jnp.float32) + sbuf[:, :, cols].astype(jnp.float32)
+        ).astype(jnp.bfloat16)
+        for d in (2, 1, 3):
+            copy = remote(
+                tbuf.at[lax.rem(at.zh + d, 4), :, cols], zbuf.at[d - 1, :, cols],
+                z_send.at[n, d], z_recv.at[n, d], at.dev(dzh=d),
+            )
+            copy.start()
+            sums.append(copy)
+    power = jnp.zeros((16, 1), jnp.float32)
+    for n in range(CHUNKS):
+        cols = pl.ds(n * CHUNK, CHUNK)
+        for copy in sums[3 * n:3 * n + 3]:
+            copy.wait_recv()
+        total = pbuf[at.k, at.zh, :, cols].astype(jnp.float32) + sbuf[at.zh, :, cols].astype(jnp.float32)
+        for d in range(3):
+            total += zbuf[d, :, cols].astype(jnp.float32)
+        total += res[:, cols].astype(jnp.float32)
+        state_ref[:, cols] = total
+        power += jnp.sum(total * total, axis=-1, keepdims=True)
+    scale = lax.rsqrt(power / WIDTH + EPSILON)
+    for n in range(CHUNKS):
+        cols = pl.ds(n * CHUNK, CHUNK)
+        normed_ref[:, cols] = (state_ref[:, cols] * scale * gain_ref[:, cols]).astype(jnp.bfloat16)
+
+    for copy in kv + qs[1:] + swaps + sums:
+        copy.wait_send()
+    for j in range(1, 8):
+        for copy in back(j):
+            copy.wait_send()
+
+
+def attention_call(query, keys, values, resid, norm_gain, out_weight):
+    vmem, hbm = pl.BlockSpec(memory_space=pltpu.VMEM), pl.BlockSpec(memory_space=pl.ANY)
+    bf, dma = jnp.bfloat16, pltpu.SemaphoreType.DMA
+    return pl.pallas_call(
+        attention_kernel,
+        name="attention",
+        out_shape=(jax.ShapeDtypeStruct((16, WIDTH), jnp.float32), jax.ShapeDtypeStruct((16, WIDTH), bf)),
+        in_specs=[vmem, vmem, vmem, hbm, vmem, hbm],
+        out_specs=(vmem, vmem),
+        scratch_shapes=[
+            pltpu.VMEM((4, 128, 256), bf), pltpu.VMEM((4, 128, 256), bf), pltpu.VMEM((8, 128, 256), bf),
+            pltpu.VMEM((8, 256, 128), bf), pltpu.VMEM((8, 8, 128), jnp.float32),
+            pltpu.VMEM((8, 256, 128), bf), pltpu.VMEM((8, 8, 128), jnp.float32),
+            pltpu.VMEM((256, WIDTH), bf), pltpu.VMEM((16, WIDTH), bf), pltpu.VMEM((256, 128), bf),
+            pltpu.VMEM((2, 4, 16, WIDTH), bf), pltpu.VMEM((4, 16, WIDTH), bf), pltpu.VMEM((4, 16, WIDTH), bf),
+            pltpu.VMEM((3, 16, WIDTH), bf),
+            dma((2, 4)), dma((2, 4)), dma((8,)), dma((8,)), dma((8,)), dma((8,)), dma((8,)), dma((8,)),
+            dma((CHUNKS,)), dma((CHUNKS,)), dma((CHUNKS, 4)), dma((CHUNKS, 4)), dma((2,)),
+        ],
+        compiler_params=pltpu.CompilerParams(
+            collective_id=1, has_side_effects=True, vmem_limit_bytes=40 << 20
+        ),
+    )(query, keys, values, resid, norm_gain.reshape(1, WIDTH), out_weight)
+
+
 EXPERTS = 64
 TOP = 6
 CAP = 2
-
-
-NEGATIVE = -1e30
-EPSILON = 1e-05
-
-
-def root_norm(hidden_state, norm_gain):
-    power = jnp.mean(hidden_state * hidden_state, axis=-1, keepdims=True)
-    return (hidden_state * lax.rsqrt(power + EPSILON) * norm_gain).astype(jnp.bfloat16)
-
 
 def slot_ranks(route_ids, text_rows):
     blocks, row_count, top_count = route_ids.shape
@@ -70,47 +264,9 @@
     ctx_rows = query.shape[0]
     row_count = ctx_rows // expert_count
     model_width = resid.shape[1]
-    local_heads = query.shape[1] // HEAD_DIM
-    score_scale = 1.0 / math.sqrt(HEAD_DIM)
-    query_spot = context_index * ctx_rows + jnp.arange(ctx_rows, dtype=jnp.int32)
-    query_heads = query.reshape(ctx_rows, local_heads, HEAD_DIM)
-    running_max = jnp.full((local_heads, ctx_rows), NEGATIVE, jnp.float32)
-    key_part = lax.all_gather(keys, "ctx", axis=0, tiled=True)
-    value_part = lax.all_gather(values, "ctx", axis=0, tiled=True)
-    amount = key_part.shape[0]
-    key_heads = key_part.reshape(amount, local_heads, HEAD_DIM)
-    value_heads = value_part.reshape(amount, local_heads, HEAD_DIM)
-    scores = (
-        jnp.einsum("qhd,khd->hqk", query_heads, key_heads, preferred_element_type=jnp.float32)
-        * score_scale
-    )
-    allowed = jnp.arange(amount, dtype=jnp.int32)[None, :] <= query_spot[:, None]
-    scores = jnp.where(allowed[None], scores, NEGATIVE)
-    new_max = jnp.maximum(running_max, jnp.max(scores, axis=-1))
-    weights = jnp.where(allowed[None], jnp.exp(scores - new_max[..., None]), 0.0)
-    running_sum = jnp.sum(weights, axis=-1)
-    running_out = jnp.einsum(
-        "hqk,khd->hqd",
-        weights.astype(jnp.bfloat16),
-        value_heads,
-        preferred_element_type=jnp.float32,
-    )
-    running_max, running_sum, running_out = (new_max, running_sum, running_out)
-    attended = (
-        (running_out / running_sum[..., None])
-        .transpose(1, 0, 2)
-        .reshape(ctx_rows, local_heads * HEAD_DIM)
-        .astype(jnp.bfloat16)
-    )
+    state_own, normed_own = attention_call(query, keys, values, resid, norm_gain, out_weight)
+    normed = lax.all_gather(normed_own, "exp", axis=0, tiled=True)
     own_start = expert_index * row_count
-    head_total = lax.psum(
-        jnp.dot(attended, out_weight, preferred_element_type=jnp.float32).astype(jnp.bfloat16),
-        "exp",
-    ).astype(jnp.float32)
-    hidden_state = resid.astype(jnp.float32) + head_total
-    normed = root_norm(hidden_state, norm_gain)
-    state_own = lax.dynamic_slice_in_dim(hidden_state, own_start, row_count, 0)
-    normed_own = lax.dynamic_slice_in_dim(normed, own_start, row_count, 0)
     image_gate, image_up, image_down = (
         lax.all_gather(img_gate, "exp", axis=0, tiled=True),
         lax.all_gather(img_up, "exp", axis=0, tiled=True),

time: 925 us -> 588 us (0.64)
  waiting for transfers between devices: 827 us -> 464 us
  Pallas kernels: 0 us -> 47.4 us
    all_gather x2 -> x1, waiting for transfers between devices: 262 us -> 21.1 us  [body(): normed = lax.all_gather(normed_own, 'exp', axis=0, tiled=True)]
    psum x1 -> x0, waiting for transfers between devices: 96 us -> none  [body(): lax.psum(jnp.dot(attended, out_weight, preferred_element_type=jnp.float32...]
    all_to_all x1, waiting for transfers between devices: 65.5 us -> 0.01 us  [body(): lax.all_to_all(outgoing, 'ctx', split_axis=0, concat_axis=0, tiled=True)]
    pallas_call x0 -> x1, Pallas kernels: none -> 47.4 us  [attention_call(): pl.pallas_call(attention_kernel, name='attention', out_shape=(jax.ShapeDt...]
    all_gather x1, waiting for transfers between devices: 119 us -> 150 us  [body(): portion = lax.all_gather(normed_own, 'ctx', axis=0, tiled=True)]
    all_gather x1, waiting for transfers between devices: 0.02 us -> 24.7 us  [body(): lax.all_gather(img_gate, 'exp', axis=0, tiled=True)]
    all_gather x1, waiting for transfers between devices: 49.4 us -> 28.3 us  [body(): lax.all_gather(img_down, 'exp', axis=0, tiled=True)]
  transfers between devices with their start and end apart: 11 -> 9, of which waited for: 9 -> 7; matrix products, arithmetic and copies ran while one was open for 5% -> 7% of each run, Pallas kernels for 0% -> 0%
where the time goes in v1:
time: 588 us; the launch traced here: 587 us
  waiting for transfers between devices  464 us (79%)
  Pallas kernels  47.4 us (8%)
  matrix products  37.3 us (6%)
  between operations  13.6 us (2%)
  starting transfers between devices  12.4 us (2%)
  local copies, waits for them, and re-layouts  7.72 us (1%)
    all_gather x1, waiting for transfers between devices, body(): portion = lax.all_gather(normed_own, 'ctx', axis=0, tiled=True)  150 us
    reduce_scatter x1, waiting for transfers between devices, body(): lax.psum_scatter(lax.dot_general(portion, image_down, (((1,), (1,)), ((),...  142 us
    reduce_scatter x1, waiting for transfers between devices, body(): lax.psum_scatter(lax.dot_general(portion, returned_flat, (((0,), (0,)), (...  59.5 us
    pallas_call x1, Pallas kernels, attention_call(): pl.pallas_call(attention_kernel, name='attention', out_shape=(jax.ShapeDt...  47.4 us
    all_gather x1, waiting for transfers between devices, body(): lax.all_gather(img_up, 'exp', axis=0, tiled=True)  36.3 us
    all_gather x1, waiting for transfers between devices, body(): lax.all_gather(img_down, 'exp', axis=0, tiled=True)  28.3 us
    all_gather x1, waiting for transfers between devices, body(): lax.all_gather(img_gate, 'exp', axis=0, tiled=True)  24.7 us
    all_gather x1, waiting for transfers between devices, body(): normed = lax.all_gather(normed_own, 'exp', axis=0, tiled=True)  21.1 us
  transfers between devices with their start and end apart: 9, of which 7 were waited for; matrix products, arithmetic and copies ran while one was open for 7% of the time, Pallas kernels for 0%

profile of v1, /device:TPU:1, one launch (start us, length us, event | category | flops | bytes accessed | tf_op | source)
XLA Modules:
  0.0 586.6 jit_solution(6434786800002975720)
XLA Ops:
  6.6 1.7 copy-done.1
  8.3 1.2 copy-done.2
  9.5 0.8 copy-done.3
  10.4 0.8 copy-done.4
  11.2 0.8 copy-done.5
  12.0 0.7 copy-done.6
  12.8 47.4 %attention.1 = (f32[16,4096]{1,0:T(8,128)S(1)}, bf16[16,4096]{1,0:T(8,128)(2,1)}) custom-call(bf16[128,256]{1,0:T(8,128)(2,1)S(1)} %copy-done.3, bf16[128,256]{1,0:T(8,128)(2,1)S(1)} %copy-done.4, bf16[128,256]{1,0:T(8,128)(2,1)S(1)} %copy-done.5, bf16[128,4096]{1,0:T(8,128)(2,1)S(1)} %copy-done.2, f32[1,4096]{1,0:T(1,128)S(1)} %bitcast.87, ...), custom_call_target="tpu_custom_call" | custom-call | tf_op jit(solution)/shard_map/attention/pallas_call | solution.py:191
  62.4 2.1 select_reduce_fusion.1
  65.1 21.1 %all-gather.14.cloned.1.call-done = bf16[128,4096]{1,0:T(8,128)(2,1)} async-done(((bf16[16,4096]{1,0:T(8,128)(2,1)}), bf16[128,4096]{1,0:T(8,128)(2,1)}) %all-gather.14.cloned.1.call-update) | async-done | bytes 1048592 | tf_op jit(solution)/shard_map/all_gather | solution.py:268
  86.3 4.4 convolution_convert_fusion
  90.7 7.1 %all-to-all-start = ((bf16[32,1,16,4096]{3,2,1,0:T(8,128)(2,1)}), bf16[32,1,16,4096]{3,2,1,0:T(8,128)(2,1)}, u32[]{:S(2)}, u32[]{:S(2)}) async-start(bf16[32,1,16,4096]{3,2,1,0:T(8,128)(2,1)} %bitcast.88), calls=%async_computation.1 | async-start | bytes 8388608 | tf_op jit(solution)/shard_map/all_to_all | solution.py:316
  99.0 24.7 %all-gather.8.cloned.1.call-done = bf16[4096,172]{0,1:T(8,128)(2,1)} async-done(((bf16[512,172]{0,1:T(8,128)(2,1)}), bf16[4096,172]{0,1:T(8,128)(2,1)}) %all-gather.8.cloned.1.call-update) | async-done | bytes 1409040 | tf_op jit(solution)/shard_map/all_gather | solution.py:271
  123.7 149.6 %all-gather.6.cloned.1.call-done = bf16[512,4096]{1,0:T(8,128)(2,1)} async-done(((bf16[16,4096]{1,0:T(8,128)(2,1)}), bf16[512,4096]{1,0:T(8,128)(2,1)}) %all-gather.6.cloned.1.call-update) | async-done | bytes 4194320 | tf_op jit(solution)/shard_map/all_gather | solution.py:276
  273.4 4.9 fusion.64
  278.3 6.4 %fusion.9 = f32[32,1,16,352]{3,2,0,1:T(8,128)} fusion(bf16[1,4096,352]{1,2,0:T(8,128)(2,1)} %param.27, bf16[32,1,16,4096]{3,2,1,0:T(8,128)(2,1)} %all-to-all-done), kind=kOutput, calls=%fused_computation.15 | convolution fusion | flops 1476395008 | bytes 7798784 | tf_op jit(solution)/shard_map/clmd,ldf->clmf/dot_general | solution.py:235
  284.7 9.7 %fusion = bf16[32,1,16,4096]{3,2,1,0:T(8,128)(2,1)} fusion(bf16[1,352,4096]{2,1,0:T(8,128)(2,1)S(1)} %copy-done, bf16[1,4096,352]{1,2,0:T(8,128)(2,1)} %param.28, bf16[32,1,16,4096]{3,2,1,0:T(8,128)(2,1)} %all-to-all-done, f32[32,1,16,352]{3,2,0,1:T(8,128)} %fusion.9), kind=kOutput, calls=%fused_computation.3 | convolution fusion | flops 2955968512 | bytes 14876672 | tf_op jit(solution)/shard_map/clmf,lfd->clmd/dot_general | solution.py:238
  294.4 4.9 all-to-all-start.1
  299.3 28.3 %all-gather.12.cloned.1.call-done = bf16[4096,172]{0,1:T(8,128)(2,1)} async-done(((bf16[512,172]{0,1:T(8,128)(2,1)}), bf16[4096,172]{0,1:T(8,128)(2,1)}) %all-gather.12.cloned.1.call-update) | async-done | bytes 1409040 | tf_op jit(solution)/shard_map/all_gather | solution.py:273
  327.6 36.3 %all-gather.10.cloned.1.call-done = bf16[4096,172]{0,1:T(8,128)(2,1)} async-done(((bf16[512,172]{0,1:T(8,128)(2,1)}), bf16[4096,172]{0,1:T(8,128)(2,1)}) %all-gather.10.cloned.1.call-update) | async-done | bytes 1409040 | tf_op jit(solution)/shard_map/all_gather | solution.py:272
  363.9 8.0 %convolution_convert_fusion.1 = bf16[512,4096]{1,0:T(8,128)(2,1)} fusion(bf16[4096,172]{0,1:T(8,128)(2,1)} %all-gather.12.cloned.1.call-done, bf16[512,4096]{1,0:T(8,128)(2,1)} %all-gather.6.cloned.1.call-done, bf16[4096,172]{0,1:T(8,128)(2,1)} %all-gather.10.cloned.1.call-done, f32[512,172]{0,1:T(8,128)} %fusion.64), kind=kOutput, calls=%fused_computation.1 | convolution fusion | flops 1445466112 | bytes 11558912 | tf_op jit(solution)/shard_map/dot_general | solution.py:282
  372.7 3.9 convolution_convert_fusion.3
  376.8 141.7 %reduce-scatter.3.cloned.1.call-done = bf16[16,4096]{1,0:T(8,128)(2,1)} async-done(((bf16[512,4096]{1,0:T(8,128)(2,1)}), bf16[16,4096]{1,0:T(8,128)(2,1)}) %reduce-scatter.3.cloned.1.call-update) | async-done | bytes 131088 | tf_op jit(solution)/shard_map/reduce_scatter | solution.py:281
  518.5 59.5 %reduce-scatter.5.cloned.1.call-done = bf16[16,4096]{1,0:T(8,128)(2,1)} async-done(((bf16[128,4096]{1,0:T(8,128)(2,1)}), bf16[16,4096]{1,0:T(8,128)(2,1)}) %reduce-scatter.5.cloned.1.call-update) | async-done | bytes 131088 | tf_op jit(solution)/shard_map/reduce_scatter | solution.py:328
  578.0 1.7 add_convert_fusion
  (48 shorter events, 4.9 us)
Async XLA Ops:
  6.5 278.1 %copy-start = (bf16[1,352,4096]{2,1,0:T(8,128)(2,1)S(1)}, bf16[1,352,4096]{2,1,0:T(8,128)(2,1)}, u32[]{:S(2)}) copy-start(bf16[1,352,4096]{2,1,0:T(8,128)(2,1)} %param.29) | copy-start | bytes 8650756
  6.5 55.1 %copy-start.7 = (s32[128,6]{0,1:T(8,128)S(1)}, s32[128,6]{0,1:T(8,128)}, u32[]{:S(2)}) copy-start(s32[128,6]{0,1:T(8,128)} %param.20) | copy-start | bytes 9220
  6.5 55.5 %copy-start.9 = (s32[128]{0:T(128)S(1)}, s32[128]{0:T(128)}, u32[]{:S(2)}) copy-start(s32[128]{0:T(128)} %param.19) | copy-start | bytes 1540
  6.5 79.7 %all-gather.14.cloned.1.call-start = ((), (), s32[]{:S(2)}) async-start(), calls=%async_computation.9 | async-start | bytes 1179648 | tf_op jit(solution)/shard_map/all_gather | solution.py:268
  6.5 1.7 copy-start.1
  8.3 1.2 copy-start.2
  9.5 0.8 copy-start.3
  10.4 0.8 copy-start.4
  11.2 0.8 copy-start.5
  12.0 0.7 copy-start.6
  60.2 63.5 %all-gather.8.cloned.1.call-start = ((), (), s32[]{:S(2)}) async-start(), calls=%async_computation.5 | async-start | bytes 1622016 | tf_op jit(solution)/shard_map/all_gather | solution.py:271
  60.9 212.4 %all-gather.6.cloned.1.call-start = ((), (), s32[]{:S(2)}) async-start(), calls=%async_computation.4 | async-start | bytes 4325376 | tf_op jit(solution)/shard_map/all_gather | solution.py:276
  90.7 187.5 %all-to-all-start = ((bf16[32,1,16,4096]{3,2,1,0:T(8,128)(2,1)}), bf16[32,1,16,4096]{3,2,1,0:T(8,128)(2,1)}, u32[]{:S(2)}, u32[]{:S(2)}) async-start(bf16[32,1,16,4096]{3,2,1,0:T(8,128)(2,1)} %bitcast.88), calls=%async_computation.1 | async-start | bytes 8388608 | tf_op jit(solution)/shard_map/all_to_all | solution.py:316
  97.9 229.7 %all-gather.12.cloned.1.call-start = ((), (), s32[]{:S(2)}) async-start(), calls=%async_computation.7 | async-start | bytes 1622016 | tf_op jit(solution)/shard_map/all_gather | solution.py:273
  98.4 265.5 %all-gather.10.cloned.1.call-start = ((), (), s32[]{:S(2)}) async-start(), calls=%async_computation.6 | async-start | bytes 1622016 | tf_op jit(solution)/shard_map/all_gather | solution.py:272
  294.4 78.4 %all-to-all-start.1 = ((bf16[32,1,16,4096]{3,2,1,0:T(8,128)(2,1)}), bf16[32,1,16,4096]{3,2,1,0:T(8,128)(2,1)}, u32[]{:S(2)}, u32[]{:S(2)}) async-start(bf16[32,1,16,4096]{3,2,1,0:T(8,128)(2,1)} %fusion), calls=%async_computation.2 | async-start | bytes 8388608 | tf_op jit(solution)/shard_map/all_to_all | solution.py:314
  299.3 219.2 %reduce-scatter.3.cloned.1.call-start = ((), (), s32[]{:S(2)}) async-start(), calls=%async_computation.8 | async-start | bytes 4325376 | tf_op jit(solution)/shard_map/reduce_scatter | solution.py:281
  371.9 0.7 copy-start.8
  371.9 206.1 %reduce-scatter.5.cloned.1.call-start = ((), (), s32[]{:S(2)}) async-start(), calls=%async_computation.10 | async-start | bytes 1179648 | tf_op jit(solution)/shard_map/reduce_scatter | solution.py:328
Sparse Core Ops, SparseCore 0:
  60.3 25.9 all-gather.13
  88.1 35.5 all-gather.7
  125.5 147.7 all-gather.5
  275.0 52.5 all-gather.11
  329.3 34.5 all-gather.9
  372.0 146.3 reduce-scatter.2
  521.0 56.9 reduce-scatter.4

commit v2 on v1

--- a/solution.py
+++ b/solution.py
@@ -210,131 +210,433 @@
     )(query, keys, values, resid, norm_gain.reshape(1, WIDTH), out_weight)
 
 
-EXPERTS = 64
-TOP = 6
-CAP = 2
-
-def slot_ranks(route_ids, text_rows):
-    blocks, row_count, top_count = route_ids.shape
-    flat = route_ids.reshape(blocks, row_count * top_count)
-    usable = jnp.broadcast_to(text_rows[:, :, None], (blocks, row_count, top_count)).reshape(
-        blocks, row_count * top_count
+def ring(at, dz, dk=0):
+    z = lax.rem(at.z + dz + 8, 8)
+    return (lax.rem(z, 2) * 16 + at.x * 4 + at.y, lax.div(z, 2) * 2 + lax.rem(at.k + dk, 2))
+
+
+def selection(at, meta, send_map, back_map):
+    lane = lax.broadcasted_iota(jnp.int32, (16, 128), 1)
+    spot = lax.broadcasted_iota(jnp.int32, (16, 128), 0)
+    to_x = lax.rem(at.x + lax.div(spot, 4), 4)
+    to_y = lax.rem(at.y + lax.rem(spot, 4), 4)
+    expert = (2 * (at.zl * 16 + to_x * 4 + to_y) + lax.div(at.zh, 2)).astype(jnp.float32)
+    chosen = jnp.zeros((16, 128), jnp.float32)
+    gate = jnp.zeros((16, 128), jnp.float32)
+    for j in range(6):
+        hit = jnp.where(meta[j:j + 1, :] == expert, 1.0, 0.0)
+        chosen += hit
+        gate += hit * meta[6 + j:7 + j, :]
+    image = jnp.broadcast_to(meta[12:13, :], (16, 128))
+    chosen = jnp.where(image == 0.0, chosen, 0.0)
+    gate = jnp.where(image == 0.0, gate, 0.0)
+    row = lax.broadcasted_iota(jnp.int32, (128, 128), 0)
+    col = lax.broadcasted_iota(jnp.int32, (128, 128), 1)
+    earlier = jnp.where((lax.div(row, 16) == lax.div(col, 16)) & (row < col), 1.0, 0.0).astype(jnp.bfloat16)
+    rank = jnp.dot(
+        jnp.concatenate([chosen, image], axis=0).astype(jnp.bfloat16), earlier, preferred_element_type=jnp.float32
     )
-    onehot = (flat[:, :, None] == jnp.arange(EXPERTS, dtype=jnp.int32)[None, None, :]) & usable[
-        :, :, None
-    ]
-    counts = jnp.cumsum(onehot.astype(jnp.int32), axis=1)
-    slot_rank = jnp.sum(jnp.where(onehot, counts, 0), axis=2) - 1
-    return (
-        slot_rank.reshape(blocks, row_count, top_count),
-        usable.reshape(blocks, row_count, top_count),
-    )
-
-
-def expert_apply(batch, exp_gate, exp_up, exp_down):
-    gate_part = jnp.einsum("clmd,ldf->clmf", batch, exp_gate, preferred_element_type=jnp.float32)
-    up_part = jnp.einsum("clmd,ldf->clmf", batch, exp_up, preferred_element_type=jnp.float32)
-    active = (jax.nn.silu(gate_part) * up_part).astype(jnp.bfloat16)
-    return jnp.einsum(
-        "clmf,lfd->clmd", active, exp_down, preferred_element_type=jnp.float32
-    ).astype(jnp.bfloat16)
+    sub = lax.div(lane, 16)
+    text_slot = (2 * sub).astype(jnp.float32) + rank[0:16]
+    text_slot = jnp.where(chosen > 0.0, text_slot, -1.0)
+    mine = (image > 0.0) & (lax.div(sub, 2) == at.zh)
+    image_slot = jnp.where(mine, (8 * (sub - 2 * at.zh)).astype(jnp.float32) + rank[16:32], -1.0)
+    slot = spot.astype(jnp.float32)
+    image_map = jnp.where(image_slot == slot, 1.0, 0.0).astype(jnp.bfloat16)
+    for t in range(16):
+        match = text_slot[t:t + 1, :] == slot
+        send_map[t, 0:16, :] = jnp.where(match, 1.0, 0.0).astype(jnp.bfloat16)
+        send_map[t, 16:32, :] = image_map
+        back_map[t, 0:16, :] = jnp.where(match, gate[t:t + 1, :], 0.0).astype(jnp.bfloat16)
+        back_map[t, 16:32, :] = image_map
+
+
+def active(gate, up):
+    return (gate / (1.0 + jnp.exp(-gate)) * up).astype(jnp.bfloat16)
+
+
+def nt_dot(a, b):
+    return lax.dot_general(a, b, (((1,), (1,)), ((), ())), preferred_element_type=jnp.float32)
+
+
+def ffn_kernel(
+    normed_ref, state_ref, meta_ref, eg_ref, eu_ref, ed_ref, iw_ref,
+    out_ref,
+    wg, wu, wd, wi, other, send_map, back_map, rows, dsend, xs, acc, ysend, ys, zsum, zsend, zrecv, tail_send, tail_recv,
+    w_send, w_recv, w_local, m_send, m_recv, p_send, p_recv, r_send, r_recv, d_send, d_recv,
+    i_send, i_recv, f_send, f_recv, t_send, t_recv, y_send, y_recv, e_send, e_recv, l_send, l_recv,
+):
+    at = Place()
+    z, k, zh = at.z, at.k, at.zh
+    p = lax.rem(at.zl + k, 2)
+    s = 1 - 2 * k
+    even, odd = p == 0, p == 1
+    chunk = [pl.ds(n * CHUNK, CHUNK) for n in range(CHUNKS)]
+    pending = []
+
+    weights = []
+    for i, (src, dst) in enumerate(((eg_ref, wg), (eu_ref, wu), (ed_ref, wd))):
+        copy = pltpu.make_async_copy(src.at[0], dst.at[0], w_local.at[i])
+        copy.start()
+        weights.append(copy)
+    barrier = pltpu.get_barrier_semaphore()
+    partners = [at.dev(dk=1), ring(at, 1), ring(at, 7)] + [at.dev(dzh=d) for d in (1, 2, 3)]
+    partners += [at.dev(dx=t // 4, dy=t % 4) for t in range(1, 16)]
+    for device in partners:
+        pl.semaphore_signal(barrier, inc=1, device_id=device, device_id_type=MESH)
+    wi[at.e] = iw_ref[...]
+    pl.semaphore_wait(barrier, len(partners))
+
+    meta_copy = remote(meta_ref, other, m_send, m_recv, at.dev(dzl=1))
+    meta_copy.start()
+
+    def pair_copy(n):
+        return remote(
+            normed_ref.at[:, chunk[n]], rows.at[zh, k, :, chunk[n]], p_send.at[n], p_recv.at[n], at.dev(dk=1)
+        )
+
+    def pair_arrival(n):
+        return remote(
+            normed_ref.at[:, chunk[n]], rows.at[zh, 1 - k, :, chunk[n]], p_send.at[n], p_recv.at[n], at.dev(dk=1)
+        )
+
+    def ring_copy(side, i, n):
+        step = (2 * i + p) * s
+        origin = lax.rem(z - step + 16, 8) if side == 0 else lax.rem(z + step + 16, 8)
+        part = rows.at[lax.div(origin, 2), :, :, chunk[n]]
+        return remote(part, part, r_send.at[side, i, n], r_recv.at[side, i, n], ring(at, s if side == 0 else -s))
+
+    def ring_arrival(side, i, n):
+        step = (2 * i + 2 - p) * s
+        origin = lax.rem(z - step + 16, 8) if side == 0 else lax.rem(z + step + 16, 8)
+        part = rows.at[lax.div(origin, 2), :, :, chunk[n]]
+        return remote(part, part, r_send.at[side, i, n], r_recv.at[side, i, n], ring(at, s if side == 0 else -s))
+
+    def plane(t, back=False):
+        dx, dy = lax.div(t, 4), lax.rem(t, 4)
+        return at.dev(dx=4 - dx, dy=4 - dy) if back else at.dev(dx=dx, dy=dy)
+
+    def row_copy(t, n):
+        return remote(dsend.at[t, :, chunk[n]], xs.at[t, :, chunk[n]], d_send.at[t, n], d_recv.at[t, n], plane(t))
+
+    @pl.when(odd)
+    def _():
+        for n in range(CHUNKS):
+            pair_copy(n).start()
+
+    @pl.when(even)
+    def _():
+        rows[zh, k] = normed_ref[...]
+
+    def stage_0(n):
+        @pl.when(even)
+        def _():
+            pair_arrival(n).wait_recv()
+            ring_copy(0, 0, n).start()
+            ring_copy(1, 0, n).start()
+
+    def stage_1(n):
+        for side in range(2):
+            ring_arrival(side, 0, n).wait_recv()
+
+            @pl.when(even)
+            def _():
+                ring_copy(side, 1, n).start()
+
+            @pl.when(odd)
+            def _():
+                ring_copy(side, 0, n).start()
+
+    def stage_2(n):
+        ring_arrival(0, 1, n).wait_recv()
+
+        @pl.when(odd)
+        def _():
+            ring_copy(0, 1, n).start()
+            ring_arrival(1, 1, n).wait_recv()
+
+    def stage_3(n):
+        part = rows[:, :, :, chunk[n]].reshape(128, CHUNK)
+        picked = jnp.dot(
+            send_map[...].reshape(512, 128), part, preferred_element_type=jnp.float32
+        ).astype(jnp.bfloat16).reshape(16, 32, CHUNK)
+        dsend[:, :, chunk[n]] = picked
+        xs[0, :, chunk[n]] = picked[0]
+
+        def go(t, _):
+            row_copy(t, n).start()
+            return 0
+
+        lax.fori_loop(1, 16, go, 0)
+
+    stage_0(0)
+    meta_copy.wait_recv()
+    selection(at, jnp.where(even, meta_ref[...], other[...]), send_map, back_map)
+    for step in range(1, CHUNKS + 3):
+        if step < CHUNKS:
+            stage_0(step)
+        if 0 <= step - 1 < CHUNKS:
+            stage_1(step - 1)
+        if 0 <= step - 2 < CHUNKS:
+            stage_2(step - 2)
+            stage_3(step - 2)
+    for i, (src, dst) in enumerate(((eg_ref, wg), (eu_ref, wu), (ed_ref, wd))):
+        copy = remote(src.at[0], dst.at[1], w_send.at[i], w_recv.at[i], at.dev(dk=1))
+        copy.start()
+        pending.append(copy)
+    swap = pending[:]
+
+    own = wi.at[at.e]
+    image_copies = [remote(own, own, i_send.at[0], i_recv.at[0], at.dev(dk=1))]
+    image_copies += [remote(own, own, i_send.at[d], i_recv.at[d], at.dev(dzh=d)) for d in (1, 2, 3)]
+    for copy in image_copies:
+        copy.start()
+
+    def image_piece(origin):
+        return wi.at[origin]
+
+    def image_arrival(d):
+        part = wi.at[2 * lax.rem(zh + 4 - d, 4) + k]
+        return remote(part, part, i_send.at[d], i_recv.at[d], at.dev(dzh=d))
+
+    def image_pass(d):
+        part = wi.at[2 * lax.rem(zh + 4 - d, 4) + k]
+        return remote(part, part, f_send.at[d], f_recv.at[d], at.dev(dk=1))
+
+    def image_pass_arrival(d):
+        part = wi.at[2 * lax.rem(zh + 4 - d, 4) + 1 - k]
+        return remote(part, part, f_send.at[d], f_recv.at[d], at.dev(dk=1))
+
+    for copy in weights[:2]:
+        copy.wait()
+    for copy in swap[:2]:
+        copy.wait_recv()
+    for n in range(CHUNKS):
+        def arrive(t, _):
+            row_copy(t, n).wait_recv()
+            return 0
+
+        lax.fori_loop(1, 16, arrive, 0)
+        part = xs[:, 0:16, chunk[n]].reshape(256, CHUNK)
+        for q in range(2):
+            for i, w in enumerate((wg, wu)):
+                term = jnp.dot(part, w[q, n * CHUNK:(n + 1) * CHUNK, :], preferred_element_type=jnp.float32)
+                if n == 0:
+                    acc[q, i] = term
+                else:
+                    acc[q, i] += term
+    acts = [active(acc[q, 0], acc[q, 1]) for q in range(2)]
+    weights[2].wait()
+    swap[2].wait_recv()
+
+    def text_back(t, n):
+        return remote(
+            ysend.at[t, 0:16, chunk[n]], ys.at[t, 0:16, chunk[n]], t_send.at[t, n], t_recv.at[t, n], plane(t, True)
+        )
+
+    def image_back(t, n):
+        return remote(
+            ysend.at[t, 16:32, chunk[n]], ys.at[t, 16:32, chunk[n]], y_send.at[t, n], y_recv.at[t, n], plane(t, True)
+        )
+
+    def send_back(result, low, n, copy):
+        result = result.astype(jnp.bfloat16).reshape(16, 16, CHUNK)
+        ysend[:, low:low + 16, chunk[n]] = result
+        ys[0, low:low + 16, chunk[n]] = result[0]
+
+        def go(t, _):
+            copy(t, n).start()
+            return 0
+
+        lax.fori_loop(1, 16, go, 0)
+
+    for n in range(CHUNKS):
+        result = jnp.dot(acts[0], wd[0, :, chunk[n]], preferred_element_type=jnp.float32)
+        result += jnp.dot(acts[1], wd[1, :, chunk[n]], preferred_element_type=jnp.float32)
+        send_back(result, 0, n, text_back)
+
+    for d in (1, 3, 2):
+        image_arrival(d).wait_recv()
+        image_pass(d).start()
+    remote(own, wi.at[2 * zh + 1 - k], i_send.at[0], i_recv.at[0], at.dev(dk=1)).wait_recv()
+    for d in (1, 3, 2):
+        image_pass_arrival(d).wait_recv()
+    gate = jnp.zeros((256, 176), jnp.float32)
+    up = jnp.zeros((256, 176), jnp.float32)
+    for e in range(8):
+        part = xs[:, 16:32, e * 512:(e + 1) * 512].reshape(256, 512)
+        gate += nt_dot(part, wi[e, 0])
+        up += nt_dot(part, wi[e, 1])
+    image_act = active(gate, up)
+    for n in range(CHUNKS):
+        result = jnp.concatenate(
+            [jnp.dot(image_act, wi[e, 2], preferred_element_type=jnp.float32) for e in (2 * n, 2 * n + 1)], axis=1
+        )
+        send_back(result, 16, n, image_back)
+
+    def sum_copy(side, i, n):
+        return remote(
+            zsend.at[side, i, :, chunk[n]], zrecv.at[side, i, :, chunk[n]],
+            e_send.at[side, i, n], e_recv.at[side, i, n], ring(at, -s if side == 0 else s),
+        )
+
+    def pass_sum(side, i, n, distance, arrival):
+        step = distance * s
+        target = lax.div(lax.rem(z - step + 16, 8) if side == 0 else lax.rem(z + step + 16, 8), 2)
+        value = zsum[target, :, chunk[n]]
+        if arrival is not None:
+            sum_copy(side, arrival, n).wait_recv()
+            value += zrecv[side, arrival, :, chunk[n]].astype(jnp.float32)
+        zsend[side, i, :, chunk[n]] = value.astype(jnp.bfloat16)
+        sum_copy(side, i, n).start()
+
+    def tail_copy(n):
+        return remote(tail_send.at[:, chunk[n]], tail_recv.at[:, chunk[n]], l_send.at[n], l_recv.at[n], at.dev(dk=1))
+
+    def end_0(n):
+        def arrive(t, _):
+            text_back(t, n).wait_recv()
+            image_back(t, n).wait_recv()
+            return 0
+
+        lax.fori_loop(1, 16, arrive, 0)
+        total = lax.dot_general(
+            back_map[...].reshape(512, 128), ys[:, :, chunk[n]].reshape(512, CHUNK),
+            (((0,), (0,)), ((), ())), preferred_element_type=jnp.float32,
+        )
+        zsum[:, :, chunk[n]] = total.reshape(4, 32, CHUNK)
+
+        @pl.when(even)
+        def _():
+            pass_sum(0, 0, n, 4, None)
+
+        @pl.when(odd)
+        def _():
+            pass_sum(1, 0, n, 3, None)
+
+    def end_1(n):
+        @pl.when(odd)
+        def _():
+            pass_sum(0, 0, n, 3, 0)
+
+        @pl.when(even)
+        def _():
+            pass_sum(1, 1, n, 2, 0)
+
+    def end_2(n):
+        @pl.when(even)
+        def _():
+            pass_sum(0, 1, n, 2, 0)
+
+        @pl.when(odd)
+        def _():
+            pass_sum(1, 1, n, 1, 1)
+
+    def end_3(n):
+        @pl.when(odd)
+        def _():
+            pass_sum(0, 1, n, 1, 1)
+
+    def end_4(n):
+        @pl.when(even)
+        def _():
+            sum_copy(0, 1, n).wait_recv()
+            sum_copy(1, 1, n).wait_recv()
+            total = zsum[zh, :, chunk[n]] + zrecv[0, 1, :, chunk[n]].astype(jnp.float32)
+            total += zrecv[1, 1, :, chunk[n]].astype(jnp.float32)
+            first, second = total[0:16], total[16:32]
+            tail_send[:, chunk[n]] = jnp.where(k == 0, second, first).astype(jnp.bfloat16)
+            tail_copy(n).start()
+            mine = jnp.where(k == 0, first, second)
+            out_ref[:, chunk[n]] = (state_ref[:, chunk[n]] + mine).astype(jnp.bfloat16)
+
+    def end_5(n):
+        @pl.when(odd)
+        def _():
+            tail_copy(n).wait_recv()
+            out_ref[:, chunk[n]] = (
+                state_ref[:, chunk[n]] + tail_recv[:, chunk[n]].astype(jnp.float32)
+            ).astype(jnp.bfloat16)
+
+    ends = (end_0, end_1, end_2, end_3, end_4, end_5)
+    for step in range(CHUNKS + len(ends) - 1):
+        for i, end in enumerate(ends):
+            if 0 <= step - i < CHUNKS:
+                end(step - i)
+
+    meta_copy.wait_send()
+    for copy in pending + image_copies:
+        copy.wait_send()
+    for d in (1, 2, 3):
+        image_pass(d).wait_send()
+    for n in range(CHUNKS):
+        def sent(t, _):
+            row_copy(t, n).wait_send()
+            text_back(t, n).wait_send()
+            image_back(t, n).wait_send()
+            return 0
+
+        lax.fori_loop(1, 16, sent, 0)
+
+        @pl.when(even)
+        def _():
+            for side, i in ((0, 0), (1, 0), (0, 1), (1, 1)):
+                ring_copy(side, i, n).wait_send()
+            for side, i in ((0, 0), (0, 1), (1, 1)):
+                sum_copy(side, i, n).wait_send()
+            tail_copy(n).wait_send()
+
+        @pl.when(odd)
+        def _():
+            pair_copy(n).wait_send()
+            for side, i in ((0, 0), (1, 0), (0, 1)):
+                ring_copy(side, i, n).wait_send()
+            for side, i in ((0, 0), (1, 0), (0, 1), (1, 1)):
+                sum_copy(side, i, n).wait_send()
+
+
+def ffn_call(normed, state, meta, exp_gate, exp_up, exp_down, image_weights):
+    vmem, hbm = pl.BlockSpec(memory_space=pltpu.VMEM), pl.BlockSpec(memory_space=pl.ANY)
+    bf, dma = jnp.bfloat16, pltpu.SemaphoreType.DMA
+    two = [dma((16, CHUNKS)), dma((16, CHUNKS))]
+    return pl.pallas_call(
+        ffn_kernel,
+        name="feed_forward",
+        out_shape=jax.ShapeDtypeStruct((16, WIDTH), bf),
+        in_specs=[vmem, vmem, vmem, hbm, hbm, hbm, vmem],
+        out_specs=vmem,
+        scratch_shapes=[
+            pltpu.VMEM((2, WIDTH, 352), bf), pltpu.VMEM((2, WIDTH, 352), bf), pltpu.VMEM((2, 352, WIDTH), bf),
+            pltpu.VMEM((8, 3, 176, 512), bf), pltpu.VMEM((16, 128), jnp.float32),
+            pltpu.VMEM((16, 32, 128), bf), pltpu.VMEM((16, 32, 128), bf),
+            pltpu.VMEM((4, 2, 16, WIDTH), bf), pltpu.VMEM((16, 32, WIDTH), bf), pltpu.VMEM((16, 32, WIDTH), bf),
+            pltpu.VMEM((2, 2, 256, 352), jnp.float32),
+            pltpu.VMEM((16, 32, WIDTH), bf), pltpu.VMEM((16, 32, WIDTH), bf),
+            pltpu.VMEM((4, 32, WIDTH), jnp.float32),
+            pltpu.VMEM((2, 2, 32, WIDTH), bf), pltpu.VMEM((2, 2, 32, WIDTH), bf),
+            pltpu.VMEM((16, WIDTH), bf), pltpu.VMEM((16, WIDTH), bf),
+            dma((3,)), dma((3,)), dma((3,)), dma, dma, dma((CHUNKS,)), dma((CHUNKS,)),
+            dma((2, 2, CHUNKS)), dma((2, 2, CHUNKS)), *two,
+            dma((4,)), dma((4,)), dma((4,)), dma((4,)), *two, *two,
+            dma((2, 2, CHUNKS)), dma((2, 2, CHUNKS)), dma((CHUNKS,)), dma((CHUNKS,)),
+        ],
+        compiler_params=pltpu.CompilerParams(
+            collective_id=2, has_side_effects=True, vmem_limit_bytes=56 << 20
+        ),
+    )(normed, state, meta, exp_gate, exp_up, exp_down, image_weights)
 
 
 def body(
-    query,
-    keys,
-    values,
-    resid,
-    flags,
-    routes,
-    gates,
-    out_weight,
-    norm_gain,
-    img_gate,
-    img_up,
-    img_down,
-    exp_gate,
-    exp_up,
-    exp_down,
+    query, keys, values, resid, flags, routes, gates, out_weight, norm_gain,
+    img_gate, img_up, img_down, exp_gate, exp_up, exp_down,
 ):
-    context_count = lax.axis_size("ctx")
-    expert_count = lax.axis_size("exp")
-    context_index = lax.axis_index("ctx")
-    expert_index = lax.axis_index("exp")
-    ctx_rows = query.shape[0]
-    row_count = ctx_rows // expert_count
-    model_width = resid.shape[1]
-    state_own, normed_own = attention_call(query, keys, values, resid, norm_gain, out_weight)
-    normed = lax.all_gather(normed_own, "exp", axis=0, tiled=True)
-    own_start = expert_index * row_count
-    image_gate, image_up, image_down = (
-        lax.all_gather(img_gate, "exp", axis=0, tiled=True),
-        lax.all_gather(img_up, "exp", axis=0, tiled=True),
-        lax.all_gather(img_down, "exp", axis=0, tiled=True),
-    )
-    own_flags = lax.dynamic_slice_in_dim(flags, own_start, row_count, 0)
-    portion = lax.all_gather(normed_own, "ctx", axis=0, tiled=True)
-    gate_part = jnp.dot(portion, image_gate, preferred_element_type=jnp.float32)
-    up_part = jnp.dot(portion, image_up, preferred_element_type=jnp.float32)
-    image_act = (jax.nn.silu(gate_part) * up_part).astype(jnp.bfloat16)
-    portion = image_act
-    image_out = lax.psum_scatter(
-        lax.dot_general(
-            portion, image_down, (((1,), (1,)), ((), ())), preferred_element_type=jnp.float32
-        ).astype(jnp.bfloat16),
-        "ctx",
-        scatter_dimension=0,
-        tiled=True,
-    ).astype(jnp.float32)
-    split_count = max(1, context_count * expert_count // EXPERTS)
-    group_count = EXPERTS // context_count
-    local_count = exp_gate.shape[0]
-    first_local = expert_index // split_count * local_count
-    text_rows = flags == 0
-    slot_rank, usable = slot_ranks(
-        routes.reshape(expert_count, row_count, TOP), text_rows.reshape(expert_count, row_count)
-    )
-    slot_rank = slot_rank.reshape(ctx_rows, TOP)
-    usable = usable.reshape(ctx_rows, TOP)
-    subset = jnp.arange(ctx_rows, dtype=jnp.int32)[:, None] // row_count
-    target = routes // group_count
-    local_id = routes % group_count - first_local
-    valid = usable & (local_id >= 0) & (local_id < local_count)
-    slot_id = jnp.where(
-        valid, ((target * local_count + local_id) * expert_count + subset) * CAP + slot_rank, -1
-    )
-    slot_total = context_count * local_count * expert_count * CAP
-    matches = slot_id[None] == jnp.arange(slot_total, dtype=jnp.int32)[:, None, None]
-    dispatch = jnp.any(matches, axis=-1).astype(jnp.bfloat16)
-    weighting = jnp.sum(jnp.where(matches, gates[None].astype(jnp.float32), 0.0), axis=-1).astype(
-        jnp.bfloat16
-    )
-    outgoing = jnp.dot(dispatch, normed, preferred_element_type=jnp.float32).astype(jnp.bfloat16)
-    outgoing = outgoing.reshape(context_count, local_count, expert_count * CAP, model_width)
-    returned = lax.all_to_all(
-        expert_apply(
-            lax.all_to_all(outgoing, "ctx", split_axis=0, concat_axis=0, tiled=True),
-            exp_gate,
-            exp_up,
-            exp_down,
-        ),
-        "ctx",
-        split_axis=0,
-        concat_axis=0,
-        tiled=True,
-    )
-    returned_flat = returned.reshape(slot_total, model_width)
-    portion = weighting
-    text_out = lax.psum_scatter(
-        lax.dot_general(
-            portion, returned_flat, (((0,), (0,)), ((), ())), preferred_element_type=jnp.float32
-        ).astype(jnp.bfloat16),
-        "exp",
-        scatter_dimension=0,
-        tiled=True,
-    ).astype(jnp.float32)
-    layer_out = state_own + jnp.where(own_flags[:, None] == 1, image_out, text_out)
-    return layer_out.astype(jnp.bfloat16)
+    meta = jnp.concatenate(
+        [routes.astype(jnp.float32), gates.astype(jnp.float32), flags.astype(jnp.float32)[:, None],
+         jnp.zeros((flags.shape[0], 3), jnp.float32)], axis=1,
+    ).T
+    image_weights = jnp.pad(jnp.stack([img_gate.T, img_up.T, img_down.T]), ((0, 0), (0, 4), (0, 0)))
+    state, normed = attention_call(query, keys, values, resid, norm_gain, out_weight)
+    return ffn_call(normed, state, meta, exp_gate, exp_up, exp_down, image_weights)
 
 
 def solution(mesh):

time: 588 us -> 208 us (0.35)
  waiting for transfers between devices: 464 us -> 0 us
  Pallas kernels: 47.4 us -> 187 us
  matrix products: 37.3 us -> 0 us
  between operations: 13.6 us -> 0.04 us
  starting transfers between devices: 12.4 us -> 0 us
  local copies, waits for them, and re-layouts: 7.72 us -> 16.5 us
    all_gather x5 -> x0, waiting for transfers between devices: 260 us -> none  [the longest x1 150 us: body(): portion = lax.all_gather(normed_own, 'ctx', axis=0, tiled=True)]
    reduce_scatter x2 -> x0, waiting for transfers between devices: 201 us -> none  [the longest x1 142 us: body(): lax.psum_scatter(lax.dot_general(portion, image_down, (((1,), (1,)), ((),...]
    pallas_call x0 -> x1, Pallas kernels: none -> 140 us  [ffn_call(): pl.pallas_call(ffn_kernel, name='feed_forward', out_shape=jax.ShapeDtypeS...]
    dot_general x6 -> x0, matrix products: 37.3 us -> none  [the longest x1 9.71 us: expert_apply(): jnp.einsum('clmf,lfd->clmd', active, exp_down, preferred_element_type=jnp...]
    all_to_all x2 -> x0, starting transfers between devices: 12 us -> none  [the longest x1 7.11 us: body(): lax.all_to_all(outgoing, 'ctx', split_axis=0, concat_axis=0, tiled=True)]
    unnamed x21 -> x25, local copies, waits for them, and re-layouts: 6.92 us -> 16.4 us
  transfers between devices with their start and end apart: 9 -> 0, of which waited for: 7 -> 0; matrix products, arithmetic and copies ran while one was open for 7% -> 0% of each run, Pallas kernels for 0% -> 0%
where the time goes in v2:
time: 208 us
  Pallas kernels  187 us (90%)
  local copies, waits for them, and re-layouts  16.5 us (8%)
  other arithmetic  4.46 us (2%)
    pallas_call x1, Pallas kernels, ffn_call(): pl.pallas_call(ffn_kernel, name='feed_forward', out_shape=jax.ShapeDtypeS...  140 us
    pallas_call x1, Pallas kernels, attention_call(): pl.pallas_call(attention_kernel, name='attention', out_shape=(jax.ShapeDt...  46.7 us
    unnamed x25, local copies, waits for them, and re-layouts  16.4 us

profile of v2, /device:TPU:1, one launch (start us, length us, event | category | flops | bytes accessed | tf_op | source)
XLA Modules:
  0.0 207.7 jit_solution(5505107430991533954)
XLA Ops:
  0.0 0.7 convert_bitcast_fusion
  0.7 0.1 pad.11.clone
  0.7 0.7 convert_element_type.11
  1.4 0.7 convert_element_type.12
  2.1 0.6 maximum_bitcast_fusion.meta_ref
  2.8 0.0 copy-start
  2.8 1.6 copy-done
  4.4 1.2 copy-done.1
  5.6 0.8 copy-done.4
  6.4 0.8 copy-done.5
  7.3 0.8 copy-done.6
  8.1 0.7 copy-done.7
  8.8 46.7 %attention.1 = (f32[16,4096]{1,0:T(8,128)S(1)}, bf16[16,4096]{1,0:T(8,128)(2,1)S(1)}) custom-call(bf16[128,256]{1,0:T(8,128)(2,1)S(1)} %copy-done.4, bf16[128,256]{1,0:T(8,128)(2,1)S(1)} %copy-done.5, bf16[128,256]{1,0:T(8,128)(2,1)S(1)} %copy-done.6, bf16[128,4096]{1,0:T(8,128)(2,1)S(1)} %copy-done.1, f32[1,4096]{1,0:T(1,128)S(1)} %bitcast.14, ...), custom_call_target="tpu_custom_call" | custom-call | tf_op jit(solution)/shard_map/attention/pallas_call | solution.py:191
  55.6 0.0 copy-start.2
  55.6 0.7 copy-done.2
  56.3 0.7 copy-done.3
  56.9 0.0 copy-done.9
  56.9 0.0 copy-done.10
  56.9 1.8 fusion.4.iw_ref
  58.7 0.0 copy-done.8
  58.7 2.8 %copy.16.eg_ref = bf16[1,4096,352]{2,1,0:T(8,128)(2,1)} copy(bf16[1,4096,352]{1,2,0:T(8,128)(2,1)S(1)} %copy-done.8) | data formatting | bytes 5767168 | tf_op args[12]
  61.5 4.6 %copy.17.eu_ref = bf16[1,4096,352]{2,1,0:T(8,128)(2,1)} copy(bf16[1,4096,352]{1,2,0:T(8,128)(2,1)} %param.28) | data formatting | bytes 5767168 | tf_op args[13]
  66.1 140.0 %feed_forward.1 = bf16[16,4096]{1,0:T(8,128)(2,1)} custom-call(bf16[16,4096]{1,0:T(8,128)(2,1)} %copy-done.3, f32[16,4096]{1,0:T(8,128)} %copy-done.2, f32[16,128]{1,0:T(8,128)} %maximum_bitcast_fusion.meta_ref, bf16[1,4096,352]{2,1,0:T(8,128)(2,1)} %copy.16.eg_ref, bf16[1,4096,352]{2,1,0:T(8,128)(2,1)} %copy.17.eu_ref, bf16[1,352,4096]{2,1,0:T(8,128)(2,1)} %ed_ref.1, ...), custom_call_target="tpu_custom_call" | custom-call | tf_op jit(solution)/shard_map/feed_forward/pallas_call | solution.py:602
  206.1 1.6 copy.19
  (10 shorter events, 0.0 us)
Async XLA Ops:
  2.8 1.6 copy-start
  4.4 1.2 copy-start.1
  5.6 0.8 copy-start.4
  6.4 0.8 copy-start.5
  7.3 0.8 copy-start.6
  8.1 0.7 copy-start.7
  8.8 48.1 %copy-start.9 = (bf16[512,172]{0,1:T(8,128)(2,1)S(1)}, bf16[512,172]{0,1:T(8,128)(2,1)}, u32[]{:S(2)}) copy-start(bf16[512,172]{0,1:T(8,128)(2,1)} %param.26) | copy-start | bytes 528388
  8.8 48.1 %copy-start.10 = (bf16[512,172]{0,1:T(8,128)(2,1)S(1)}, bf16[512,172]{0,1:T(8,128)(2,1)}, u32[]{:S(2)}) copy-start(bf16[512,172]{0,1:T(8,128)(2,1)} %param.25) | copy-start | bytes 528388
  8.8 49.9 %copy-start.8 = (bf16[1,4096,352]{1,2,0:T(8,128)(2,1)S(1)}, bf16[1,4096,352]{1,2,0:T(8,128)(2,1)}, u32[]{:S(2)}) copy-start(bf16[1,4096,352]{1,2,0:T(8,128)(2,1)} %param.27) | copy-start | bytes 8650756
  55.6 0.7 copy-start.2
  56.3 0.7 copy-start.3

commit v3 on v0

v3 whole, which is shorter than its diff:
```python
import math

import jax
import jax.numpy as jnp
from jax import lax
from jax.experimental import pallas as pl
from jax.experimental.pallas import tpu as pltpu
from jax.sharding import PartitionSpec as P

MESH = pl.DeviceIdType.MESH
HEAD_DIM = 128
NEGATIVE = -1e30
EPSILON = 1e-05
WIDTH = 4096
CHUNK = 1024
CHUNKS = WIDTH // CHUNK
BF16 = jnp.bfloat16
F32 = jnp.float32


class Place:
    def __init__(self):
        c, e = lax.axis_index("ctx"), lax.axis_index("exp")
        self.e = e
        self.zl, self.x, self.y = lax.div(c, 16), lax.rem(lax.div(c, 4), 4), lax.rem(c, 4)
        self.zh, self.k = lax.div(e, 2), lax.rem(e, 2)
        self.z = self.zh * 2 + self.zl

    def dev(self, dx=0, dy=0, dzl=0, dzh=0, dk=0):
        x, y = lax.rem(self.x + dx + 4, 4), lax.rem(self.y + dy + 4, 4)
        zl, zh, k = lax.rem(self.zl + dzl, 2), lax.rem(self.zh + dzh + 4, 4), lax.rem(self.k + dk, 2)
        return (zl * 16 + x * 4 + y, zh * 2 + k)

    def column(self, dz, core):
        z = lax.rem(self.z + dz, 8)
        return (lax.rem(z, 2) * 16 + self.x * 4 + self.y, lax.div(z, 2) * 2 + core)

    def plane(self, t, back=False):
        dx, dy = lax.div(t, 4), lax.rem(t, 4)
        return self.dev(dx=4 - dx, dy=4 - dy) if back else self.dev(dx=dx, dy=dy)


def remote(src, dst, send, recv, device):
    return pltpu.make_async_remote_copy(
        src_ref=src, dst_ref=dst, send_sem=send, recv_sem=recv, device_id=device, device_id_type=MESH
    )


def nt_dot(a, b):
    return lax.dot_general(a, b, (((1,), (1,)), ((), ())), preferred_element_type=F32)


def tn_dot(a, b):
    return lax.dot_general(a, b, (((0,), (0,)), ((), ())), preferred_element_type=F32)


def pieces(value):
    first = value.astype(BF16).astype(F32)
    second = (value - first).astype(BF16).astype(F32)
    return [first, second, value - first - second]


def active(gate, up):
    return (gate / (1.0 + jnp.exp(-gate)) * up).astype(BF16)


def each(low, high, step):
    def go(t, carried):
        step(t)
        return carried

    lax.fori_loop(low, high, go, 0)


def selection(at, meta, text_map, back_map, image_map):
    lane = lax.broadcasted_iota(jnp.int32, (16, 128), 1)
    spot = lax.broadcasted_iota(jnp.int32, (16, 128), 0)
    to_x = lax.rem(at.x + lax.div(spot, 4), 4)
    to_y = lax.rem(at.y + lax.rem(spot, 4), 4)
    expert = (2 * (at.zl * 16 + to_x * 4 + to_y) + lax.div(at.zh, 2)).astype(F32)
    chosen = jnp.zeros((16, 128), F32)
    gate = jnp.zeros((16, 128), F32)
    for j in range(6):
        hit = jnp.where(meta[j:j + 1, :] == expert, 1.0, 0.0)
        chosen += hit
        gate += hit * meta[6 + j:7 + j, :]
    image = jnp.broadcast_to(meta[12:13, :], (16, 128))
    chosen = jnp.where(image == 0.0, chosen, 0.0)
    gate = jnp.where(image == 0.0, gate, 0.0)
    row = lax.broadcasted_iota(jnp.int32, (128, 128), 0)
    col = lax.broadcasted_iota(jnp.int32, (128, 128), 1)
    earlier = jnp.where((lax.div(row, 16) == lax.div(col, 16)) & (row < col), 1.0, 0.0).astype(BF16)
    rank = jnp.dot(jnp.concatenate([chosen, image], axis=0).astype(BF16), earlier, preferred_element_type=F32)
    sub = lax.div(lane, 16)
    text_slot = jnp.where(chosen > 0.0, (2 * sub).astype(F32) + rank[0:16], -1.0)
    mine = (image > 0.0) & (lax.div(sub, 2) == at.zh)
    image_slot = jnp.where(mine, (8 * (sub - 2 * at.zh)).astype(F32) + rank[16:32], -1.0)
    slot = spot.astype(F32)
    image_map[...] = jnp.where(image_slot == slot, 1.0, 0.0).astype(BF16)
    for t in range(16):
        match = text_slot[t:t + 1, :] == slot
        text_map[16 * t:16 * t + 16, :] = jnp.where(match, 1.0, 0.0).astype(BF16)
        back_map[16 * t:16 * t + 16, :] = jnp.where(match, gate[t:t + 1, :], 0.0).astype(BF16)


def layer_kernel(
    q_ref, k_ref, v_ref, resid_ref, flags_ref, routes_ref, gates_ref, ow_ref, gain_ref,
    ig_ref, iu_ref, id_ref, eg_ref, eu_ref, ed_ref,
    out_ref,
    kbuf, vbuf, qbuf, obuf, rbuf, ow, res, att, pbuf, sbuf, tbuf, zbuf, state, normed,
    wg, wu, wd, wi, meta, other, text_map, back_map, image_map, rows, tsend, xt, xi, acc,
    ysend, ys, isend, ir1, is2, ir2, zsend, zrecv, zown,
    kv_send, kv_recv, q_send, q_recv, o_send, o_recv, c_send, c_recv, z_send, z_recv, local_sem,
    w_send, w_recv, m_send, m_recv, g_send, g_recv, d_send, d_recv, x1_send, x1_recv, x2_send, x2_recv,
    i_send, i_recv, f_send, f_recv, t_send, t_recv, y1_send, y1_recv, y2_send, y2_recv, e_send, e_recv,
):
    at = Place()
    z, k, zh, zl = at.z, at.k, at.zh, at.zl
    p = lax.rem(zl + k, 2)
    even, odd = p == 0, p == 1
    chunk = [pl.ds(n * CHUNK, CHUNK) for n in range(CHUNKS)]
    heads = [pl.ds(h * HEAD_DIM, HEAD_DIM) for h in range(2)]

    def load(i, src, dst):
        copy = pltpu.make_async_copy(src, dst, local_sem.at[i])
        copy.start()
        return copy

    own_kv = []
    for h in range(2):
        own_kv.append([
            load(3 * h, q_ref.at[:, heads[h]], qbuf.at[h, 0]),
            load(3 * h + 1, k_ref.at[:, heads[h]], kbuf.at[h, 0]),
            load(3 * h + 2, v_ref.at[:, heads[h]], vbuf.at[h, 0]),
        ])
    own_rows = pl.ds(pl.multiple_of(at.e * 16, 16), 16)
    load_r = load(6, resid_ref.at[own_rows], res)
    load_w = load(7, ow_ref, ow)
    barrier = pltpu.get_barrier_semaphore()
    partners = [at.plane(t) for t in range(1, 16)]
    partners += [at.column(dz, lax.rem(k + dk, 2)) for dz in range(8) for dk in range(2) if (dz, dk) != (0, 0)]
    partners += [at.dev(dzl=1, dy=d) for d in (1, 2, 3)]
    for device in partners:
        pl.semaphore_signal(barrier, inc=1, device_id=device, device_id_type=MESH)
    meta[0:6, :] = routes_ref[...].astype(F32)
    meta[6:12, :] = gates_ref[...].astype(F32)
    meta[12:16, :] = jnp.broadcast_to(flags_ref[...].astype(F32), (4, 128))
    pad = jnp.zeros((4, 512), BF16)
    for i, ref in enumerate((ig_ref, iu_ref, id_ref)):
        wi[at.e, i] = jnp.concatenate([ref[...], pad], axis=0)
    pl.semaphore_wait(barrier, len(partners))

    def q_copy(h, j):
        dy, dzl = lax.rem(j, 4), lax.div(j, 4)
        return remote(q_ref.at[:, heads[h]], qbuf.at[h, j], q_send.at[h, j], q_recv.at[h, j], at.dev(dzl=dzl, dy=dy))

    kv = []
    for h in range(2):
        each(1, 8, lambda j: q_copy(h, j).start())
        kv.append([])
        for d in (1, 3, 2):
            for i, (ref, buf) in enumerate(((k_ref, kbuf), (v_ref, vbuf))):
                copy = remote(ref.at[:, heads[h]], buf.at[h, d], kv_send.at[i, h, d], kv_recv.at[i, h, d], at.dev(dx=d))
                copy.start()
                kv[h].append(copy)
    meta_copy = remote(meta, other, m_send, m_recv, at.dev(dzl=1))
    meta_copy.start()
    weights, swap = [], []
    for i, (src, dst) in enumerate(((eg_ref, wg), (eu_ref, wu), (ed_ref, wd))):
        weights.append(load(8 + i, src.at[0], dst.at[0:352]))
        copy = remote(src.at[0], dst.at[352:704], w_send.at[i], w_recv.at[i], at.dev(dk=1))
        copy.start()
        swap.append(copy)

    key_row = lax.broadcasted_iota(jnp.int32, (512, 128), 0)
    lanes = lax.broadcasted_iota(jnp.int32, (512, 128), 1)
    from_x = lax.rem(at.x - lax.div(key_row, 128) + 4, 4)
    key_spot = (zl * 16 + from_x * 4 + at.y) * 128 + lax.rem(key_row, 128) - lanes

    def back(h, j):
        device = at.dev(dzl=lax.div(j, 4), dy=4 - lax.rem(j, 4))
        return remote(obuf.at[h, j], rbuf.at[h, j], o_send.at[h, j], o_recv.at[h, j], device)

    for h in range(2):
        for copy in own_kv[h]:
            copy.wait()
        for copy in kv[h]:
            copy.wait_recv()

        def one_block(j):
            @pl.when(j > 0)
            def _():
                q_copy(h, j).wait_recv()

            q_zl = lax.rem(zl + lax.div(j, 4), 2)
            q_y = lax.rem(at.y + 4 - lax.rem(j, 4), 4)
            allowed = key_spot <= (q_zl * 16 + at.x * 4 + q_y) * 128
            s = nt_dot(kbuf[h].reshape(512, HEAD_DIM), qbuf[h, j])
            s = jnp.where(allowed, s * (math.log2(math.e) / math.sqrt(HEAD_DIM)), NEGATIVE)
            m = jnp.max(s, axis=0, keepdims=True)
            w = jnp.exp2(s - m)
            l = jnp.sum(w, axis=0, keepdims=True)
            o = tn_dot(vbuf[h].reshape(512, HEAD_DIM), w.astype(BF16))
            obuf[h, j, 0:128, :] = o.astype(BF16)
            stats = pieces(m) + pieces(l) + [m, l]
            obuf[h, j, 128:144, :] = jnp.concatenate(stats + stats, axis=0).astype(BF16)

            @pl.when(j > 0)
            def _():
                back(h, j).start()

        each(0, 8, one_block)

    for h in range(2):
        rbuf[h, 0] = obuf[h, 0]
        for j in range(1, 8):
            back(h, j).wait_recv()
        stats = [rbuf[h, j, 128:144, :].astype(F32) for j in range(8)]
        tops = [st[0:1] + st[1:2] + st[2:3] for st in stats]
        top = tops[0]
        for j in range(1, 8):
            top = jnp.maximum(top, tops[j])
        total = jnp.zeros((HEAD_DIM, 128), F32)
        denom = jnp.zeros((1, 128), F32)
        for j in range(8):
            w = jnp.exp2(tops[j] - top)
            denom += w * (stats[j][3:4] + stats[j][4:5] + stats[j][5:6])
            total += w * rbuf[h, j, 0:128, :].astype(F32)
        att[h * HEAD_DIM:(h + 1) * HEAD_DIM, :] = (total / denom).astype(BF16)

    load_w.wait()
    load_r.wait()
    swaps, sums = [], []
    for n in range(CHUNKS):
        part = tn_dot(att[...], ow[:, chunk[n]]).astype(BF16)
        for b in range(8):
            pbuf[b % 2, b // 2, :, chunk[n]] = part[16 * b:16 * b + 16]
        copy = remote(pbuf.at[1 - k, :, :, chunk[n]], sbuf.at[:, :, chunk[n]], c_send.at[n], c_recv.at[n], at.dev(dk=1))
        copy.start()
        swaps.append(copy)
    for n in range(CHUNKS):
        swaps[n].wait_recv()
        tbuf[:, :, chunk[n]] = (
            pbuf[k, :, :, chunk[n]].astype(F32) + sbuf[:, :, chunk[n]].astype(F32)
        ).astype(BF16)
        for d in (2, 1, 3):
            copy = remote(
                tbuf.at[lax.rem(zh + d, 4), :, chunk[n]], zbuf.at[d - 1, :, chunk[n]],
                z_send.at[n, d], z_recv.at[n, d], at.dev(dzh=d),
            )
            copy.start()
            sums.append(copy)
    meta_copy.wait_recv()
    selection(at, jnp.where(even, meta[...], other[...]), text_map, back_map, image_map)
    power = jnp.zeros((16, 1), F32)
    for n in range(CHUNKS):
        for copy in sums[3 * n:3 * n + 3]:
            copy.wait_recv()
        total = pbuf[k, zh, :, chunk[n]].astype(F32) + sbuf[zh, :, chunk[n]].astype(F32)
        for d in range(3):
            total += zbuf[d, :, chunk[n]].astype(F32)
        total += res[:, chunk[n]].astype(F32)
        state[:, chunk[n]] = total
        power += jnp.sum(total * total, axis=-1, keepdims=True)
    scale = lax.rsqrt(power / WIDTH + EPSILON)
    for n in range(CHUNKS):
        normed[:, chunk[n]] = (state[:, chunk[n]] * scale * gain_ref[:, chunk[n]]).astype(BF16)

    def gather(dz, n):
        return remote(
            normed.at[:, chunk[n]], rows.at[zh, k, :, chunk[n]],
            g_send.at[dz, n], g_recv.at[dz, k, n], at.column(dz, zl),
        )

    def gathered(dz, core, n):
        origin = lax.div(lax.rem(z - dz + 8, 8), 2)
        part = rows.at[origin, core, :, chunk[n]]
        return remote(part, part, g_send.at[dz, n], g_recv.at[dz, core, n], at.column(dz, zl))

    for n in range(CHUNKS):
        @pl.when(odd)
        def _():
            gather(0, n).start()

        for dz in (4, 3, 5, 2, 6, 1, 7):
            gather(dz, n).start()

    @pl.when(even)
    def _():
        rows[zh, k] = normed[...]

    own = wi.at[at.e]
    image_copies = [remote(own, own, i_send.at[0], i_recv.at[0], at.dev(dk=1))]
    image_copies += [remote(own, own, i_send.at[d], i_recv.at[d], at.dev(dzh=d)) for d in (1, 2, 3)]
    for copy in image_copies:
        copy.start()

    def text_copy(t, n):
        return remote(tsend.at[t, :, chunk[n]], xt.at[t, :, chunk[n]], d_send.at[t, n], d_recv.at[t, n], at.plane(t))

    def first_hop(d, n):
        src = xi.at[0, 0, :, chunk[n]]
        if n % 2 == 0:
            return remote(src, xi.at[0, d, :, chunk[n]], x1_send.at[d, n], x1_recv.at[d, n], at.dev(dx=d))
        return remote(src, xi.at[d, 0, :, chunk[n]], x1_send.at[d, n], x1_recv.at[d, n], at.dev(dy=d))

    def second_hop(d, n):
        if n % 2 == 0:
            src, dst, device = xi.at[0, :, :, chunk[n]], xi.at[d, :, :, chunk[n]], at.dev(dy=d)
        else:
            src, dst, device = xi.at[:, 0, :, chunk[n]], xi.at[:, d, :, chunk[n]], at.dev(dx=d)
        return remote(src, dst, x2_send.at[d, n], x2_recv.at[d, n], device)

    def dispatch(n):
        for i in range(1, 4):
            for core in range(2):
                gathered(p + 2 * i, core, n).wait_recv()

        @pl.when(even)
        def _():
            gathered(0, 1 - k, n).wait_recv()

        @pl.when(odd)
        def _():
            for core in range(2):
                gathered(1, core, n).wait_recv()

        part = rows[:, :, :, chunk[n]].reshape(128, CHUNK)
        xi[0, 0, :, chunk[n]] = jnp.dot(image_map[...], part, preferred_element_type=F32).astype(BF16)
        for d in (1, 3, 2):
            first_hop(d, n).start()
        picked = jnp.dot(text_map[...], part, preferred_element_type=F32).astype(BF16).reshape(16, 16, CHUNK)
        tsend[:, :, chunk[n]] = picked
        xt[0, :, chunk[n]] = picked[0]
        each(1, 16, lambda t: text_copy(t, n).start())

    def forward(n):
        for d in (1, 3, 2):
            first_hop(d, n).wait_recv()
        for d in (1, 3, 2):
            second_hop(d, n).start()

    for n in range(CHUNKS):
        dispatch(n)
        if n > 0:
            forward(n - 1)
    forward(CHUNKS - 1)

    for copy in weights[:2]:
        copy.wait()
    for copy in swap[:2]:
        copy.wait_recv()
    for n in range(CHUNKS):
        each(1, 16, lambda t: text_copy(t, n).wait_recv())
        part = xt[:, :, chunk[n]].reshape(256, CHUNK)
        for i, w in enumerate((wg, wu)):
            term = nt_dot(part, w[:, chunk[n]])
            if n == 0:
                acc[i] = term
            else:
                acc[i] += term
    text_act = active(acc[0], acc[1])
    weights[2].wait()
    swap[2].wait_recv()

    def text_back(t, n):
        return remote(
            ysend.at[t, :, chunk[n]], ys.at[t, :, chunk[n]], t_send.at[t, n], t_recv.at[t, n], at.plane(t, True)
        )

    for n in range(CHUNKS):
        result = jnp.dot(text_act, wd[:, chunk[n]], preferred_element_type=F32).astype(BF16).reshape(16, 16, CHUNK)
        ysend[:, :, chunk[n]] = result
        ys[0, :, chunk[n]] = result[0]
        each(1, 16, lambda t: text_back(t, n).start())

    def image_arrival(d):
        part = wi.at[2 * lax.rem(zh + 4 - d, 4) + k]
        return remote(part, part, i_send.at[d], i_recv.at[d], at.dev(dzh=d))

    def image_pass(d):
        part = wi.at[2 * lax.rem(zh + 4 - d, 4) + k]
        return remote(part, part, f_send.at[d], f_recv.at[d], at.dev(dk=1))

    def image_passed(d):
        part = wi.at[2 * lax.rem(zh + 4 - d, 4) + 1 - k]
        return remote(part, part, f_send.at[d], f_recv.at[d], at.dev(dk=1))

    for d in (1, 3, 2):
        image_arrival(d).wait_recv()
        image_pass(d).start()
    remote(own, wi.at[2 * zh + 1 - k], i_send.at[0], i_recv.at[0], at.dev(dk=1)).wait_recv()
    for d in (1, 3, 2):
        image_passed(d).wait_recv()
    gate_up = jnp.zeros((256, 352), F32)
    for n in range(CHUNKS):
        for d in (1, 3, 2):
            second_hop(d, n).wait_recv()
        for e in (2 * n, 2 * n + 1):
            part = xi[:, :, :, e * 512:(e + 1) * 512].reshape(256, 512)
            gate_up += nt_dot(part, wi[e, 0:2].reshape(352, 512))
    image_act = active(gate_up[:, 0:176], gate_up[:, 176:352])

    def sum_one(d, n):
        if n % 2 == 0:
            src, device = isend.at[d, :, :, chunk[n]], at.dev(dy=4 - d)
        else:
            src, device = isend.at[:, d, :, chunk[n]], at.dev(dx=4 - d)
        return remote(src, ir1.at[d - 1, :, :, chunk[n]], y1_send.at[d, n], y1_recv.at[d, n], device)

    def sum_two(d, n):
        device = at.dev(dx=4 - d) if n % 2 == 0 else at.dev(dy=4 - d)
        return remote(is2.at[d, :, chunk[n]], ir2.at[d - 1, :, chunk[n]], y2_send.at[d, n], y2_recv.at[d, n], device)

    def image_down(n):
        result = jnp.concatenate(
            [jnp.dot(image_act, wi[e, 2], preferred_element_type=F32) for e in (2 * n, 2 * n + 1)], axis=1
        )
        isend[:, :, :, chunk[n]] = result.astype(BF16).reshape(4, 4, 16, CHUNK)
        for d in (1, 3, 2):
            sum_one(d, n).start()

    def image_turn(n):
        total = (isend[0, :, :, chunk[n]] if n % 2 == 0 else isend[:, 0, :, chunk[n]]).astype(F32)
        for d in (1, 3, 2):
            sum_one(d, n).wait_recv()
            total += ir1[d - 1, :, :, chunk[n]].astype(F32)
        is2[:, :, chunk[n]] = total.astype(BF16)
        for d in (1, 3, 2):
            sum_two(d, n).start()

    def to_owner(i, core, n):
        dz = p + 2 * i
        target = lax.div(lax.rem(z + dz, 8), 2) * 2 + core
        return remote(
            zsend.at[target, :, chunk[n]], zrecv.at[dz, :, chunk[n]],
            e_send.at[i, core, n], e_recv.at[dz, n], at.column(dz, core),
        )

    def from_column(dz, n):
        part = zrecv.at[dz, :, chunk[n]]
        return remote(part, part, e_send.at[0, 0, n], e_recv.at[dz, n], at.column(dz, k))

    def combine(n):
        each(1, 16, lambda t: text_back(t, n).wait_recv())
        image_total = is2[0, :, chunk[n]].astype(F32)
        for d in (1, 3, 2):
            sum_two(d, n).wait_recv()
            image_total += ir2[d - 1, :, chunk[n]].astype(F32)
        total = tn_dot(back_map[...], ys[:, :, chunk[n]].reshape(256, CHUNK))
        total += tn_dot(image_map[...], image_total.astype(BF16))
        total = total.reshape(8, 16, CHUNK)
        zsend[:, :, chunk[n]] = total.astype(BF16)
        for i in (2, 1, 3):
            for core in range(2):
                to_owner(i, core, n).start()

        @pl.when(odd)
        def _():
            for core in range(2):
                to_owner(0, core, n).start()

        @pl.when(even)
        def _():
            to_owner(0, 1 - k, n).start()
            zown[:, chunk[n]] = zsend[at.e, :, chunk[n]].astype(F32)

        @pl.when(odd)
        def _():
            zown[:, chunk[n]] = jnp.zeros((16, CHUNK), F32)

    def finish(n):
        total = state[:, chunk[n]] + zown[:, chunk[n]]
        for dz in range(1, 8):
            from_column(dz, n).wait_recv()
            total += zrecv[dz, :, chunk[n]].astype(F32)
        out_ref[:, chunk[n]] = total.astype(BF16)

        @pl.when(odd)
        def _():
            from_column(0, n).wait_recv()
            out_ref[:, chunk[n]] = (total + zrecv[0, :, chunk[n]].astype(F32)).astype(BF16)

    for n in range(CHUNKS):
        image_down(n)
        if n > 0:
            image_turn(n - 1)
    image_turn(CHUNKS - 1)
    for n in range(CHUNKS):
        combine(n)
        if n > 0:
            finish(n - 1)
    finish(CHUNKS - 1)

    meta_copy.wait_send()
    for copy in kv[0] + kv[1] + swap + swaps + sums + image_copies:
        copy.wait_send()
    for h in range(2):
        def sent_a(j):
            q_copy(h, j).wait_send()
            back(h, j).wait_send()

        each(1, 8, sent_a)
    for d in (1, 2, 3):
        image_pass(d).wait_send()
    for n in range(CHUNKS):
        def sent_b(t):
            text_copy(t, n).wait_send()
            text_back(t, n).wait_send()

        each(1, 16, sent_b)
        for dz in range(1, 8):
            gather(dz, n).wait_send()
        for d in (1, 2, 3):
            first_hop(d, n).wait_send()
            second_hop(d, n).wait_send()
            sum_one(d, n).wait_send()
            sum_two(d, n).wait_send()
            for core in range(2):
                to_owner(d, core, n).wait_send()

        @pl.when(odd)
        def _():
            gather(0, n).wait_send()
            for core in range(2):
                to_owner(0, core, n).wait_send()

        @pl.when(even)
        def _():
            to_owner(0, 1 - k, n).wait_send()


def body(
    query, keys, values, resid, flags, routes, gates, out_weight, norm_gain,
    img_gate, img_up, img_down, exp_gate, exp_up, exp_down,
):
    vmem, hbm = pl.BlockSpec(memory_space=pltpu.VMEM), pl.BlockSpec(memory_space=pl.ANY)
    dma = pltpu.SemaphoreType.DMA

    def buf(*shape, dtype=BF16):
        return pltpu.VMEM(shape, dtype)

    def pair(*shape):
        return [dma(shape), dma(shape)]

    return pl.pallas_call(
        layer_kernel,
        name="layer",
        out_shape=jax.ShapeDtypeStruct((16, WIDTH), BF16),
        in_specs=[hbm] * 4 + [vmem] * 3 + [hbm, vmem] + [vmem] * 3 + [hbm] * 3,
        out_specs=vmem,
        scratch_shapes=[
            buf(2, 4, 128, 128), buf(2, 4, 128, 128), buf(2, 8, 128, 128), buf(2, 8, 144, 128), buf(2, 8, 144, 128),
            buf(256, WIDTH), buf(16, WIDTH), buf(256, 128),
            buf(2, 4, 16, WIDTH), buf(4, 16, WIDTH), buf(4, 16, WIDTH), buf(3, 16, WIDTH),
            buf(16, WIDTH, dtype=F32), buf(16, WIDTH),
            buf(704, WIDTH), buf(704, WIDTH), buf(704, WIDTH), buf(8, 3, 176, 512),
            buf(16, 128, dtype=F32), buf(16, 128, dtype=F32), buf(256, 128), buf(256, 128), buf(16, 128),
            buf(4, 2, 16, WIDTH), buf(16, 16, WIDTH), buf(16, 16, WIDTH), buf(4, 4, 16, WIDTH),
            buf(2, 256, 704, dtype=F32),
            buf(16, 16, WIDTH), buf(16, 16, WIDTH), buf(4, 4, 16, WIDTH), buf(3, 4, 16, WIDTH),
            buf(4, 16, WIDTH), buf(3, 16, WIDTH), buf(8, 16, WIDTH), buf(8, 16, WIDTH), buf(16, WIDTH, dtype=F32),
            *pair(2, 2, 4), *pair(2, 8), *pair(2, 8), *pair(CHUNKS), *pair(CHUNKS, 4), dma((11,)),
            *pair(3), dma, dma, dma((8, CHUNKS)), dma((8, 2, CHUNKS)), *pair(16, CHUNKS),
            *pair(4, CHUNKS), *pair(4, CHUNKS), *pair(4), *pair(4), *pair(16, CHUNKS),
            *pair(4, CHUNKS), *pair(4, CHUNKS), dma((4, 2, CHUNKS)), dma((8, CHUNKS)),
        ],
        compiler_params=pltpu.CompilerParams(
            collective_id=1, has_side_effects=True, vmem_limit_bytes=60 << 20
        ),
    )(
        query, keys, values, resid, flags.reshape(1, -1), routes.T, gates.T, out_weight, norm_gain.reshape(1, WIDTH),
        img_gate.T, img_up.T, img_down.T,
        exp_gate.transpose(0, 2, 1), exp_up.transpose(0, 2, 1), exp_down,
    )


def solution(mesh):
    return jax.shard_map(
        body,
        mesh=mesh,
        in_specs=(
            P("ctx", "exp"),
            P("ctx", "exp"),
            P("ctx", "exp"),
            P("ctx", None),
            P("ctx"),
            P("ctx", None),
            P("ctx", None),
            P("exp", None),
            P(),
            P("exp", "ctx"),
            P("exp", "ctx"),
            P("exp", "ctx"),
            P(("ctx", "exp"), None, None),
            P(("ctx", "exp"), None, None),
            P(("ctx", "exp"), None, None),
        ),
        out_specs=P(("ctx", "exp"), None),
        check_vma=False,
    )
```

time: 925 us -> 173 us (0.19)
  waiting for transfers between devices: 827 us -> 0 us
  Pallas kernels: 0 us -> 171 us
  matrix products: 44.7 us -> 0 us
  starting transfers between devices: 17.1 us -> 0 us
  between operations: 13.4 us -> 0.01 us
  other arithmetic: 9.79 us -> 0 us
  local copies, waits for them, and re-layouts: 10.9 us -> 1.57 us
    all_gather x6 -> x0, waiting for transfers between devices: 463 us -> none  [the longest x1 146 us: body(): value_part = lax.all_gather(values, 'ctx', axis=0, tiled=True)]
    reduce_scatter x2 -> x0, waiting for transfers between devices: 201 us -> none  [the longest x1 141 us: body(): lax.psum_scatter(lax.dot_general(portion, image_down, (((1,), (1,)), ((),...]
    pallas_call x0 -> x1, Pallas kernels: none -> 171 us  [body(): pl.pallas_call(layer_kernel, name='layer', out_shape=jax.ShapeDtypeStruct...]
    psum x1 -> x0, waiting for transfers between devices: 96 us -> none  [body(): lax.psum(jnp.dot(attended, out_weight, preferred_element_type=jnp.float32...]
    all_to_all x2 -> x0, waiting for transfers between devices: 65.5 us -> none  [the longest x1 65.5 us: body(): lax.all_to_all(outgoing, 'ctx', split_axis=0, concat_axis=0, tiled=True)]
    dot_general x9 -> x0, matrix products: 44.7 us -> none  [the longest x1 9.75 us: expert_apply(): jnp.einsum('clmf,lfd->clmd', active, exp_down, preferred_element_type=jnp...]
    all_to_all x2 -> x0, starting transfers between devices: 16.6 us -> none  [the longest x1 9.48 us: body(): lax.all_to_all(expert_apply(lax.all_to_all(outgoing, 'ctx', split_axis=0,...]
  transfers between devices with their start and end apart: 11 -> 0, of which waited for: 9 -> 0; matrix products, arithmetic and copies ran while one was open for 5% -> 0% of each run, Pallas kernels for 0% -> 0%
where the time goes in v3:
time: 173 us
  Pallas kernels  171 us (99%)
    pallas_call x1, Pallas kernels, body(): pl.pallas_call(layer_kernel, name='layer', out_shape=jax.ShapeDtypeStruct...  171 us

profile of v3, /device:TPU:1, one launch (start us, length us, event | category | flops | bytes accessed | tf_op | source)
XLA Modules:
  0.0 172.6 jit_solution(14749672089722023375)
XLA Ops:
  0.0 171.0 %layer.1 = bf16[16,4096]{1,0:T(8,128)(2,1)} custom-call(bf16[128,256]{1,0:T(8,128)(2,1)} %q_ref.1, bf16[128,256]{1,0:T(8,128)(2,1)} %k_ref.1, bf16[128,256]{1,0:T(8,128)(2,1)} %v_ref.1, bf16[128,4096]{1,0:T(8,128)(2,1)} %resid_ref.1, s32[1,128]{1,0:T(1,128)} %bitcast.17, s32[6,128]{1,0:T(8,128)} %bitcast.15, bf16[6,128]{1,0:T(8,128)(2,1)} %bitcast.16, ...), custom_call_target="tpu_custom_call" | custom-call | tf_op jit(solution)/shard_map/layer/pallas_call | solution.py:546
  171.0 1.6 copy.17

commit v4 on v3

--- a/solution.py
+++ b/solution.py
@@ -14,6 +14,8 @@
 WIDTH = 4096
 CHUNK = 1024
 CHUNKS = WIDTH // CHUNK
+SCALE = WIDTH
+WIDE = WIDTH + 128
 BF16 = jnp.bfloat16
 F32 = jnp.float32
 
@@ -32,7 +34,7 @@
         return (zl * 16 + x * 4 + y, zh * 2 + k)
 
     def column(self, dz, core):
-        z = lax.rem(self.z + dz, 8)
+        z = lax.rem(self.z + dz + 8, 8)
         return (lax.rem(z, 2) * 16 + self.x * 4 + self.y, lax.div(z, 2) * 2 + core)
 
     def plane(self, t, back=False):
@@ -111,14 +113,17 @@
     wg, wu, wd, wi, meta, other, text_map, back_map, image_map, rows, tsend, xt, xi, acc,
     ysend, ys, isend, ir1, is2, ir2, zsend, zrecv, zown,
     kv_send, kv_recv, q_send, q_recv, o_send, o_recv, c_send, c_recv, z_send, z_recv, local_sem,
-    w_send, w_recv, m_send, m_recv, g_send, g_recv, d_send, d_recv, x1_send, x1_recv, x2_send, x2_recv,
-    i_send, i_recv, f_send, f_recv, t_send, t_recv, y1_send, y1_recv, y2_send, y2_recv, e_send, e_recv,
+    w_send, w_recv, m_send, m_recv, p_send, p_recv, g_send, g_recv, d_send, d_recv, x1_send, x1_recv, x2_send, x2_recv,
+    i_send, i_recv, f_send, f_recv, h_send, h_recv, t_send, t_recv, y1_send, y1_recv, y2_send, y2_recv, e_send, e_recv,
 ):
     at = Place()
     z, k, zh, zl = at.z, at.k, at.zh, at.zl
     p = lax.rem(zl + k, 2)
     even, odd = p == 0, p == 1
+    side_step = 1 - 2 * k
     chunk = [pl.ds(n * CHUNK, CHUNK) for n in range(CHUNKS)]
+    size = [CHUNK] * (CHUNKS - 1) + [CHUNK + WIDE - WIDTH]
+    wide = [pl.ds(n * CHUNK, size[n]) for n in range(CHUNKS)]
     heads = [pl.ds(h * HEAD_DIM, HEAD_DIM) for h in range(2)]
 
     def load(i, src, dst):
@@ -252,8 +257,9 @@
             sums.append(copy)
     meta_copy.wait_recv()
     selection(at, jnp.where(even, meta[...], other[...]), text_map, back_map, image_map)
-    power = jnp.zeros((16, 1), F32)
-    for n in range(CHUNKS):
+    powers = []
+
+    def norm_step(n):
         for copy in sums[3 * n:3 * n + 3]:
             copy.wait_recv()
         total = pbuf[k, zh, :, chunk[n]].astype(F32) + sbuf[zh, :, chunk[n]].astype(F32)
@@ -261,77 +267,120 @@
             total += zbuf[d, :, chunk[n]].astype(F32)
         total += res[:, chunk[n]].astype(F32)
         state[:, chunk[n]] = total
-        power += jnp.sum(total * total, axis=-1, keepdims=True)
-    scale = lax.rsqrt(power / WIDTH + EPSILON)
-    for n in range(CHUNKS):
-        normed[:, chunk[n]] = (state[:, chunk[n]] * scale * gain_ref[:, chunk[n]]).astype(BF16)
-
-    def gather(dz, n):
+        powers.append(jnp.sum(total * total, axis=-1, keepdims=True))
+        normed[:, chunk[n]] = (total * gain_ref[:, chunk[n]]).astype(BF16)
+        if n == CHUNKS - 1:
+            scale = jnp.broadcast_to(lax.rsqrt(sum(powers) / WIDTH + EPSILON), (16, 64))
+            high = scale.astype(BF16)
+            low = (scale - high.astype(F32)).astype(BF16)
+            normed[:, SCALE:WIDE] = jnp.concatenate([high, low], axis=1)
+
+        @pl.when(odd)
+        def _():
+            pair_copy(n).start()
+
+        @pl.when(even)
+        def _():
+            rows[zh, k, :, wide[n]] = normed[:, wide[n]]
+            pair_arrival(n).wait_recv()
+            ring_copy(0, 0, n).start()
+            ring_copy(1, 0, n).start()
+
+    def pair_copy(n):
         return remote(
-            normed.at[:, chunk[n]], rows.at[zh, k, :, chunk[n]],
-            g_send.at[dz, n], g_recv.at[dz, k, n], at.column(dz, zl),
+            normed.at[:, wide[n]], rows.at[zh, k, :, wide[n]], p_send.at[n], p_recv.at[n], at.dev(dk=1)
         )
 
-    def gathered(dz, core, n):
-        origin = lax.div(lax.rem(z - dz + 8, 8), 2)
-        part = rows.at[origin, core, :, chunk[n]]
-        return remote(part, part, g_send.at[dz, n], g_recv.at[dz, core, n], at.column(dz, zl))
-
-    for n in range(CHUNKS):
+    def pair_arrival(n):
+        part = rows.at[zh, 1 - k, :, wide[n]]
+        return remote(part, part, p_send.at[n], p_recv.at[n], at.dev(dk=1))
+
+    def ring_part(side, steps, n):
+        step = steps * side_step
+        origin = lax.rem(z - step + 16, 8) if side == 0 else lax.rem(z + step + 16, 8)
+        return rows.at[lax.div(origin, 2), :, :, wide[n]]
+
+    def ring_remote(side, i, n, part):
+        device = at.column(side_step if side == 0 else -side_step, k)
+        return remote(part, part, g_send.at[side, i, n], g_recv.at[side, i, n], device)
+
+    def ring_copy(side, i, n):
+        return ring_remote(side, i, n, ring_part(side, 2 * i + p, n))
+
+    def ring_arrival(side, i, n):
+        return ring_remote(side, i, n, ring_part(side, 2 * i + 2 - p, n))
+
+    def ring_one(n):
+        for side in range(2):
+            ring_arrival(side, 0, n).wait_recv()
+
+            @pl.when(even)
+            def _():
+                ring_copy(side, 1, n).start()
+
+            @pl.when(odd)
+            def _():
+                ring_copy(side, 0, n).start()
+
+    def ring_two(n):
+        ring_arrival(0, 1, n).wait_recv()
+
         @pl.when(odd)
         def _():
-            gather(0, n).start()
-
-        for dz in (4, 3, 5, 2, 6, 1, 7):
-            gather(dz, n).start()
-
-    @pl.when(even)
-    def _():
-        rows[zh, k] = normed[...]
+            ring_copy(0, 1, n).start()
+            ring_arrival(1, 1, n).wait_recv()
 
     own = wi.at[at.e]
     image_copies = [remote(own, own, i_send.at[0], i_recv.at[0], at.dev(dk=1))]
-    image_copies += [remote(own, own, i_send.at[d], i_recv.at[d], at.dev(dzh=d)) for d in (1, 2, 3)]
-    for copy in image_copies:
-        copy.start()
+    image_copies += [remote(own, own, i_send.at[d], i_recv.at[d], at.dev(dzh=d)) for d in (1, 3)]
+
+    def image_piece(d, core):
+        return wi.at[2 * lax.rem(zh + 4 - d, 4) + core]
+
+    def image_arrival(d):
+        part = image_piece(d, k)
+        return remote(part, part, i_send.at[d], i_recv.at[d], at.dev(dzh=d))
+
+    def image_half(d):
+        part = image_piece(d, k).at[:, :, 0:256] if d == 1 else image_piece(d, k).at[:, :, 256:512]
+        return remote(part, part, h_send.at[d], h_recv.at[d], at.dev(dzh=d))
+
+    def image_half_arrival(d):
+        part = image_piece(2, k).at[:, :, 0:256] if d == 1 else image_piece(2, k).at[:, :, 256:512]
+        return remote(part, part, h_send.at[d], h_recv.at[d], at.dev(dzh=d))
+
+    def image_pass(d):
+        part = image_piece(d, k)
+        return remote(part, part, f_send.at[d], f_recv.at[d], at.dev(dk=1))
+
+    def image_passed(d):
+        part = image_piece(d, 1 - k)
+        return remote(part, part, f_send.at[d], f_recv.at[d], at.dev(dk=1))
 
     def text_copy(t, n):
-        return remote(tsend.at[t, :, chunk[n]], xt.at[t, :, chunk[n]], d_send.at[t, n], d_recv.at[t, n], at.plane(t))
+        return remote(tsend.at[t, :, wide[n]], xt.at[t, :, wide[n]], d_send.at[t, n], d_recv.at[t, n], at.plane(t))
 
     def first_hop(d, n):
-        src = xi.at[0, 0, :, chunk[n]]
+        src = xi.at[0, 0, :, wide[n]]
         if n % 2 == 0:
-            return remote(src, xi.at[0, d, :, chunk[n]], x1_send.at[d, n], x1_recv.at[d, n], at.dev(dx=d))
-        return remote(src, xi.at[d, 0, :, chunk[n]], x1_send.at[d, n], x1_recv.at[d, n], at.dev(dy=d))
+            return remote(src, xi.at[0, d, :, wide[n]], x1_send.at[d, n], x1_recv.at[d, n], at.dev(dx=d))
+        return remote(src, xi.at[d, 0, :, wide[n]], x1_send.at[d, n], x1_recv.at[d, n], at.dev(dy=d))
 
     def second_hop(d, n):
         if n % 2 == 0:
-            src, dst, device = xi.at[0, :, :, chunk[n]], xi.at[d, :, :, chunk[n]], at.dev(dy=d)
+            src, dst, device = xi.at[0, :, :, wide[n]], xi.at[d, :, :, wide[n]], at.dev(dy=d)
         else:
-            src, dst, device = xi.at[:, 0, :, chunk[n]], xi.at[:, d, :, chunk[n]], at.dev(dx=d)
+            src, dst, device = xi.at[:, 0, :, wide[n]], xi.at[:, d, :, wide[n]], at.dev(dx=d)
         return remote(src, dst, x2_send.at[d, n], x2_recv.at[d, n], device)
 
     def dispatch(n):
-        for i in range(1, 4):
-            for core in range(2):
-                gathered(p + 2 * i, core, n).wait_recv()
-
-        @pl.when(even)
-        def _():
-            gathered(0, 1 - k, n).wait_recv()
-
-        @pl.when(odd)
-        def _():
-            for core in range(2):
-                gathered(1, core, n).wait_recv()
-
-        part = rows[:, :, :, chunk[n]].reshape(128, CHUNK)
-        xi[0, 0, :, chunk[n]] = jnp.dot(image_map[...], part, preferred_element_type=F32).astype(BF16)
+        part = rows[:, :, :, wide[n]].reshape(128, size[n])
+        xi[0, 0, :, wide[n]] = jnp.dot(image_map[...], part, preferred_element_type=F32).astype(BF16)
         for d in (1, 3, 2):
             first_hop(d, n).start()
-        picked = jnp.dot(text_map[...], part, preferred_element_type=F32).astype(BF16).reshape(16, 16, CHUNK)
-        tsend[:, :, chunk[n]] = picked
-        xt[0, :, chunk[n]] = picked[0]
+        picked = jnp.dot(text_map[...], part, preferred_element_type=F32).astype(BF16).reshape(16, 16, size[n])
+        tsend[:, :, wide[n]] = picked
+        xt[0, :, wide[n]] = picked[0]
         each(1, 16, lambda t: text_copy(t, n).start())
 
     def forward(n):
@@ -340,11 +389,19 @@
         for d in (1, 3, 2):
             second_hop(d, n).start()
 
-    for n in range(CHUNKS):
-        dispatch(n)
-        if n > 0:
-            forward(n - 1)
-    forward(CHUNKS - 1)
+    for step in range(CHUNKS + 3):
+        if step < CHUNKS:
+            norm_step(step)
+        if 0 <= step - 1 < CHUNKS:
+            ring_one(step - 1)
+        if 0 <= step - 2 < CHUNKS:
+            ring_two(step - 2)
+            if step - 2 == CHUNKS - 1:
+                for copy in image_copies:
+                    copy.start()
+            dispatch(step - 2)
+        if 0 <= step - 3 < CHUNKS:
+            forward(step - 3)
 
     for copy in weights[:2]:
         copy.wait()
@@ -359,7 +416,14 @@
                 acc[i] = term
             else:
                 acc[i] += term
-    text_act = active(acc[0], acc[1])
+        if n == 2:
+            for d in (1, 3):
+                image_arrival(d).wait_recv()
+                image_half(d).start()
+                image_pass(d).start()
+    text_scale = xt[:, :, SCALE:WIDE].reshape(256, 128).astype(F32)
+    text_scale = text_scale[:, 0:1] + text_scale[:, 64:65]
+    text_act = active(acc[0] * text_scale, acc[1] * text_scale)
     weights[2].wait()
     swap[2].wait_recv()
 
@@ -368,28 +432,18 @@
             ysend.at[t, :, chunk[n]], ys.at[t, :, chunk[n]], t_send.at[t, n], t_recv.at[t, n], at.plane(t, True)
         )
 
-    for n in range(CHUNKS):
+    def text_down(n):
         result = jnp.dot(text_act, wd[:, chunk[n]], preferred_element_type=F32).astype(BF16).reshape(16, 16, CHUNK)
         ysend[:, :, chunk[n]] = result
         ys[0, :, chunk[n]] = result[0]
         each(1, 16, lambda t: text_back(t, n).start())
 
-    def image_arrival(d):
-        part = wi.at[2 * lax.rem(zh + 4 - d, 4) + k]
-        return remote(part, part, i_send.at[d], i_recv.at[d], at.dev(dzh=d))
-
-    def image_pass(d):
-        part = wi.at[2 * lax.rem(zh + 4 - d, 4) + k]
-        return remote(part, part, f_send.at[d], f_recv.at[d], at.dev(dk=1))
-
-    def image_passed(d):
-        part = wi.at[2 * lax.rem(zh + 4 - d, 4) + 1 - k]
-        return remote(part, part, f_send.at[d], f_recv.at[d], at.dev(dk=1))
-
-    for d in (1, 3, 2):
-        image_arrival(d).wait_recv()
-        image_pass(d).start()
+    text_down(0)
+    text_down(1)
     remote(own, wi.at[2 * zh + 1 - k], i_send.at[0], i_recv.at[0], at.dev(dk=1)).wait_recv()
+    for d in (1, 3):
+        image_half_arrival(d).wait_recv()
+    image_pass(2).start()
     for d in (1, 3, 2):
         image_passed(d).wait_recv()
     gate_up = jnp.zeros((256, 352), F32)
@@ -399,6 +453,8 @@
         for e in (2 * n, 2 * n + 1):
             part = xi[:, :, :, e * 512:(e + 1) * 512].reshape(256, 512)
             gate_up += nt_dot(part, wi[e, 0:2].reshape(352, 512))
+    image_scale = xi[:, :, :, SCALE:WIDE].reshape(256, 128).astype(F32)
+    gate_up = gate_up * (image_scale[:, 0:1] + image_scale[:, 64:65])
     image_act = active(gate_up[:, 0:176], gate_up[:, 176:352])
 
     def sum_one(d, n):
@@ -481,12 +537,16 @@
             from_column(0, n).wait_recv()
             out_ref[:, chunk[n]] = (total + zrecv[0, :, chunk[n]].astype(F32)).astype(BF16)
 
+    image_down(0)
+    image_down(1)
+    text_down(2)
+    image_down(2)
+    image_turn(0)
+    text_down(3)
+    image_down(3)
     for n in range(CHUNKS):
-        image_down(n)
-        if n > 0:
-            image_turn(n - 1)
-    image_turn(CHUNKS - 1)
-    for n in range(CHUNKS):
+        if n + 1 < CHUNKS:
+            image_turn(n + 1)
         combine(n)
         if n > 0:
             finish(n - 1)
@@ -503,14 +563,14 @@
         each(1, 8, sent_a)
     for d in (1, 2, 3):
         image_pass(d).wait_send()
+    for d in (1, 3):
+        image_half(d).wait_send()
     for n in range(CHUNKS):
         def sent_b(t):
             text_copy(t, n).wait_send()
             text_back(t, n).wait_send()
 
         each(1, 16, sent_b)
-        for dz in range(1, 8):
-            gather(dz, n).wait_send()
         for d in (1, 2, 3):
             first_hop(d, n).wait_send()
             second_hop(d, n).wait_send()
@@ -519,14 +579,18 @@
             for core in range(2):
                 to_owner(d, core, n).wait_send()
 
+        for side, i in ((0, 0), (1, 0), (0, 1)):
+            ring_copy(side, i, n).wait_send()
+
         @pl.when(odd)
         def _():
-            gather(0, n).wait_send()
+            pair_copy(n).wait_send()
             for core in range(2):
                 to_owner(0, core, n).wait_send()
 
         @pl.when(even)
         def _():
+            ring_copy(1, 1, n).wait_send()
             to_owner(0, 1 - k, n).wait_send()
 
 
@@ -553,16 +617,16 @@
             buf(2, 4, 128, 128), buf(2, 4, 128, 128), buf(2, 8, 128, 128), buf(2, 8, 144, 128), buf(2, 8, 144, 128),
             buf(256, WIDTH), buf(16, WIDTH), buf(256, 128),
             buf(2, 4, 16, WIDTH), buf(4, 16, WIDTH), buf(4, 16, WIDTH), buf(3, 16, WIDTH),
-            buf(16, WIDTH, dtype=F32), buf(16, WIDTH),
+            buf(16, WIDTH, dtype=F32), buf(16, WIDE),
             buf(704, WIDTH), buf(704, WIDTH), buf(704, WIDTH), buf(8, 3, 176, 512),
             buf(16, 128, dtype=F32), buf(16, 128, dtype=F32), buf(256, 128), buf(256, 128), buf(16, 128),
-            buf(4, 2, 16, WIDTH), buf(16, 16, WIDTH), buf(16, 16, WIDTH), buf(4, 4, 16, WIDTH),
+            buf(4, 2, 16, WIDE), buf(16, 16, WIDE), buf(16, 16, WIDE), buf(4, 4, 16, WIDE),
             buf(2, 256, 704, dtype=F32),
             buf(16, 16, WIDTH), buf(16, 16, WIDTH), buf(4, 4, 16, WIDTH), buf(3, 4, 16, WIDTH),
             buf(4, 16, WIDTH), buf(3, 16, WIDTH), buf(8, 16, WIDTH), buf(8, 16, WIDTH), buf(16, WIDTH, dtype=F32),
             *pair(2, 2, 4), *pair(2, 8), *pair(2, 8), *pair(CHUNKS), *pair(CHUNKS, 4), dma((11,)),
-            *pair(3), dma, dma, dma((8, CHUNKS)), dma((8, 2, CHUNKS)), *pair(16, CHUNKS),
-            *pair(4, CHUNKS), *pair(4, CHUNKS), *pair(4), *pair(4), *pair(16, CHUNKS),
+            *pair(3), dma, dma, *pair(CHUNKS), *pair(2, 2, CHUNKS), *pair(16, CHUNKS),
+            *pair(4, CHUNKS), *pair(4, CHUNKS), *pair(4), *pair(4), *pair(4), *pair(16, CHUNKS),
             *pair(4, CHUNKS), *pair(4, CHUNKS), dma((4, 2, CHUNKS)), dma((8, CHUNKS)),
         ],
         compiler_params=pltpu.CompilerParams(

time: 173 us -> 161 us (0.931)
  Pallas kernels: 171 us -> 159 us
    pallas_call x1, Pallas kernels: 171 us -> 159 us  [body(): pl.pallas_call(layer_kernel, name='layer', out_shape=jax.ShapeDtypeStruct...]
where the time goes in v4:
time: 161 us
  Pallas kernels  159 us (99%)
    pallas_call x1, Pallas kernels, body(): pl.pallas_call(layer_kernel, name='layer', out_shape=jax.ShapeDtypeStruct...  159 us

profile of v4, /device:TPU:1, one launch (start us, length us, event | category | flops | bytes accessed | tf_op | source)
XLA Modules:
  0.0 161.1 jit_solution(12985026068710160135)
XLA Ops:
  0.0 159.5 %layer.1 = bf16[16,4096]{1,0:T(8,128)(2,1)} custom-call(bf16[128,256]{1,0:T(8,128)(2,1)} %q_ref.1, bf16[128,256]{1,0:T(8,128)(2,1)} %k_ref.1, bf16[128,256]{1,0:T(8,128)(2,1)} %v_ref.1, bf16[128,4096]{1,0:T(8,128)(2,1)} %resid_ref.1, s32[1,128]{1,0:T(1,128)} %bitcast.17, s32[6,128]{1,0:T(8,128)} %bitcast.15, bf16[6,128]{1,0:T(8,128)(2,1)} %bitcast.16, ...), custom_call_target="tpu_custom_call" | custom-call | tf_op jit(solution)/shard_map/layer/pallas_call | solution.py:610
  159.5 1.6 copy.17

commit v5 on v4

--- a/solution.py
+++ b/solution.py
@@ -16,6 +16,8 @@
 CHUNKS = WIDTH // CHUNK
 SCALE = WIDTH
 WIDE = WIDTH + 128
+HALF = CHUNK // 2
+PACKED = WIDTH // 2
 BF16 = jnp.bfloat16
 F32 = jnp.float32
 
@@ -95,10 +97,11 @@
     rank = jnp.dot(jnp.concatenate([chosen, image], axis=0).astype(BF16), earlier, preferred_element_type=F32)
     sub = lax.div(lane, 16)
     text_slot = jnp.where(chosen > 0.0, (2 * sub).astype(F32) + rank[0:16], -1.0)
-    mine = (image > 0.0) & (lax.div(sub, 2) == at.zh)
-    image_slot = jnp.where(mine, (8 * (sub - 2 * at.zh)).astype(F32) + rank[16:32], -1.0)
+    mine = (image > 0.0) & (sub == at.z)
     slot = spot.astype(F32)
-    image_map[...] = jnp.where(image_slot == slot, 1.0, 0.0).astype(BF16)
+    for half in range(2):
+        image_slot = jnp.where(mine, rank[16:32] + 8.0 * half, -1.0)
+        image_map[half] = jnp.where(image_slot == slot, 1.0, 0.0).astype(BF16)
     for t in range(16):
         match = text_slot[t:t + 1, :] == slot
         text_map[16 * t:16 * t + 16, :] = jnp.where(match, 1.0, 0.0).astype(BF16)
@@ -111,10 +114,10 @@
     out_ref,
     kbuf, vbuf, qbuf, obuf, rbuf, ow, res, att, pbuf, sbuf, tbuf, zbuf, state, normed,
     wg, wu, wd, wi, meta, other, text_map, back_map, image_map, rows, tsend, xt, xi, acc,
-    ysend, ys, isend, ir1, is2, ir2, zsend, zrecv, zown,
+    ysend, ys, isend, ir1, is2, ir2, zsend, zrecv, zown, spots, spot_recv,
     kv_send, kv_recv, q_send, q_recv, o_send, o_recv, c_send, c_recv, z_send, z_recv, local_sem,
     w_send, w_recv, m_send, m_recv, p_send, p_recv, g_send, g_recv, d_send, d_recv, x1_send, x1_recv, x2_send, x2_recv,
-    i_send, i_recv, f_send, f_recv, h_send, h_recv, t_send, t_recv, y1_send, y1_recv, y2_send, y2_recv, e_send, e_recv,
+    i_send, i_recv, f_send, f_recv, t_send, t_recv, y1_send, y1_recv, y2_send, y2_recv, e_send, e_recv, s_send, s_recv,
 ):
     at = Place()
     z, k, zh, zl = at.z, at.k, at.zh, at.zl
@@ -124,6 +127,8 @@
     chunk = [pl.ds(n * CHUNK, CHUNK) for n in range(CHUNKS)]
     size = [CHUNK] * (CHUNKS - 1) + [CHUNK + WIDE - WIDTH]
     wide = [pl.ds(n * CHUNK, size[n]) for n in range(CHUNKS)]
+    half = [pl.ds(n * HALF, HALF) for n in range(CHUNKS)]
+    packed = [pl.ds(n * HALF, size[n] - HALF) for n in range(CHUNKS)]
     heads = [pl.ds(h * HEAD_DIM, HEAD_DIM) for h in range(2)]
 
     def load(i, src, dst):
@@ -152,7 +157,7 @@
     meta[12:16, :] = jnp.broadcast_to(flags_ref[...].astype(F32), (4, 128))
     pad = jnp.zeros((4, 512), BF16)
     for i, ref in enumerate((ig_ref, iu_ref, id_ref)):
-        wi[at.e, i] = jnp.concatenate([ref[...], pad], axis=0)
+        wi[zl, at.e, i] = jnp.concatenate([ref[...], pad], axis=0)
     pl.semaphore_wait(barrier, len(partners))
 
     def q_copy(h, j):
@@ -177,6 +182,33 @@
         copy.start()
         swap.append(copy)
 
+    def image_slot(dz, core):
+        place = lax.rem(z + dz + 8, 8)
+        return wi.at[lax.rem(place, 2), lax.div(place, 2) * 2 + core]
+
+    def image_ring(side, i, distance):
+        part = image_slot(distance if side else -distance, k)
+        if i == 3:
+            part = part.at[:, :, 256:512] if side else part.at[:, :, 0:256]
+        return remote(part, part, i_send.at[side, i], i_recv.at[side, i], at.column(-1 if side else 1, k))
+
+    def image_pass(dz):
+        part = image_slot(dz, k)
+        return remote(part, part, f_send.at[dz + 3], f_recv.at[dz + 3], at.dev(dk=1))
+
+    def image_passed(dz):
+        part = image_slot(dz, 1 - k)
+        return remote(part, part, f_send.at[dz + 3], f_recv.at[dz + 3], at.dev(dk=1))
+
+    def image_step(i):
+        for side in range(2):
+            image_ring(side, i - 1, i).wait_recv()
+            image_ring(side, i, i).start()
+            image_pass(i if side else -i).start()
+
+    for side in range(2):
+        image_ring(side, 0, 0).start()
+    image_pass(0).start()
     key_row = lax.broadcasted_iota(jnp.int32, (512, 128), 0)
     lanes = lax.broadcasted_iota(jnp.int32, (512, 128), 1)
     from_x = lax.rem(at.x - lax.div(key_row, 128) + 4, 4)
@@ -215,6 +247,7 @@
                 back(h, j).start()
 
         each(0, 8, one_block)
+
 
     for h in range(2):
         rbuf[h, 0] = obuf[h, 0]
@@ -330,52 +363,30 @@
             ring_copy(0, 1, n).start()
             ring_arrival(1, 1, n).wait_recv()
 
-    own = wi.at[at.e]
-    image_copies = [remote(own, own, i_send.at[0], i_recv.at[0], at.dev(dk=1))]
-    image_copies += [remote(own, own, i_send.at[d], i_recv.at[d], at.dev(dzh=d)) for d in (1, 3)]
-
-    def image_piece(d, core):
-        return wi.at[2 * lax.rem(zh + 4 - d, 4) + core]
-
-    def image_arrival(d):
-        part = image_piece(d, k)
-        return remote(part, part, i_send.at[d], i_recv.at[d], at.dev(dzh=d))
-
-    def image_half(d):
-        part = image_piece(d, k).at[:, :, 0:256] if d == 1 else image_piece(d, k).at[:, :, 256:512]
-        return remote(part, part, h_send.at[d], h_recv.at[d], at.dev(dzh=d))
-
-    def image_half_arrival(d):
-        part = image_piece(2, k).at[:, :, 0:256] if d == 1 else image_piece(2, k).at[:, :, 256:512]
-        return remote(part, part, h_send.at[d], h_recv.at[d], at.dev(dzh=d))
-
-    def image_pass(d):
-        part = image_piece(d, k)
-        return remote(part, part, f_send.at[d], f_recv.at[d], at.dev(dk=1))
-
-    def image_passed(d):
-        part = image_piece(d, 1 - k)
-        return remote(part, part, f_send.at[d], f_recv.at[d], at.dev(dk=1))
-
     def text_copy(t, n):
         return remote(tsend.at[t, :, wide[n]], xt.at[t, :, wide[n]], d_send.at[t, n], d_recv.at[t, n], at.plane(t))
 
     def first_hop(d, n):
-        src = xi.at[0, 0, :, wide[n]]
+        src = xi.at[0, 0, :, packed[n]]
         if n % 2 == 0:
-            return remote(src, xi.at[0, d, :, wide[n]], x1_send.at[d, n], x1_recv.at[d, n], at.dev(dx=d))
-        return remote(src, xi.at[d, 0, :, wide[n]], x1_send.at[d, n], x1_recv.at[d, n], at.dev(dy=d))
+            return remote(src, xi.at[0, d, :, packed[n]], x1_send.at[d, n], x1_recv.at[d, n], at.dev(dx=d))
+        return remote(src, xi.at[d, 0, :, packed[n]], x1_send.at[d, n], x1_recv.at[d, n], at.dev(dy=d))
 
     def second_hop(d, n):
         if n % 2 == 0:
-            src, dst, device = xi.at[0, :, :, wide[n]], xi.at[d, :, :, wide[n]], at.dev(dy=d)
+            src, dst, device = xi.at[0, :, :, packed[n]], xi.at[d, :, :, packed[n]], at.dev(dy=d)
         else:
-            src, dst, device = xi.at[:, 0, :, wide[n]], xi.at[:, d, :, wide[n]], at.dev(dx=d)
+            src, dst, device = xi.at[:, 0, :, packed[n]], xi.at[:, d, :, packed[n]], at.dev(dx=d)
         return remote(src, dst, x2_send.at[d, n], x2_recv.at[d, n], device)
 
     def dispatch(n):
         part = rows[:, :, :, wide[n]].reshape(128, size[n])
-        xi[0, 0, :, wide[n]] = jnp.dot(image_map[...], part, preferred_element_type=F32).astype(BF16)
+        image = jnp.dot(image_map[0], part[:, 0:HALF], preferred_element_type=F32)
+        image += jnp.dot(image_map[1], part[:, HALF:CHUNK], preferred_element_type=F32)
+        if size[n] > CHUNK:
+            factor = jnp.dot(image_map[0], part[:, CHUNK:], preferred_element_type=F32)
+            image = jnp.concatenate([image, factor], axis=1)
+        xi[0, 0, :, packed[n]] = image.astype(BF16)
         for d in (1, 3, 2):
             first_hop(d, n).start()
         picked = jnp.dot(text_map[...], part, preferred_element_type=F32).astype(BF16).reshape(16, 16, size[n])
@@ -397,8 +408,7 @@
         if 0 <= step - 2 < CHUNKS:
             ring_two(step - 2)
             if step - 2 == CHUNKS - 1:
-                for copy in image_copies:
-                    copy.start()
+                image_step(1)
             dispatch(step - 2)
         if 0 <= step - 3 < CHUNKS:
             forward(step - 3)
@@ -416,11 +426,8 @@
                 acc[i] = term
             else:
                 acc[i] += term
-        if n == 2:
-            for d in (1, 3):
-                image_arrival(d).wait_recv()
-                image_half(d).start()
-                image_pass(d).start()
+        if n == 1:
+            image_step(2)
     text_scale = xt[:, :, SCALE:WIDE].reshape(256, 128).astype(F32)
     text_scale = text_scale[:, 0:1] + text_scale[:, 64:65]
     text_act = active(acc[0] * text_scale, acc[1] * text_scale)
@@ -438,50 +445,56 @@
         ys[0, :, chunk[n]] = result[0]
         each(1, 16, lambda t: text_back(t, n).start())
 
-    text_down(0)
-    text_down(1)
-    remote(own, wi.at[2 * zh + 1 - k], i_send.at[0], i_recv.at[0], at.dev(dk=1)).wait_recv()
-    for d in (1, 3):
-        image_half_arrival(d).wait_recv()
-    image_pass(2).start()
-    for d in (1, 3, 2):
-        image_passed(d).wait_recv()
-    gate_up = jnp.zeros((256, 352), F32)
-    for n in range(CHUNKS):
-        for d in (1, 3, 2):
-            second_hop(d, n).wait_recv()
-        for e in (2 * n, 2 * n + 1):
-            part = xi[:, :, :, e * 512:(e + 1) * 512].reshape(256, 512)
-            gate_up += nt_dot(part, wi[e, 0:2].reshape(352, 512))
-    image_scale = xi[:, :, :, SCALE:WIDE].reshape(256, 128).astype(F32)
-    gate_up = gate_up * (image_scale[:, 0:1] + image_scale[:, 64:65])
-    image_act = active(gate_up[:, 0:176], gate_up[:, 176:352])
+    image_act = []
+
+    def image_ready():
+        for side in range(2):
+            image_ring(side, 3, 4).wait_recv()
+        image_pass(4).start()
+        for dz in (0, -1, 1, -2, 2, -3, 3, 4):
+            image_passed(dz).wait_recv()
+        lows = [jnp.zeros((256, 352), F32)] * 2
+        highs = [jnp.zeros((256, 352), F32)] * 2
+        for n in range(CHUNKS):
+            for d in (1, 3, 2):
+                second_hop(d, n).wait_recv()
+            part = xi[:, :, :, half[n]].reshape(256, HALF)
+            for b in range(2):
+                lows[b] += nt_dot(part, wi[b, 2 * n, 0:2].reshape(352, 512))
+                highs[b] += nt_dot(part, wi[b, 2 * n + 1, 0:2].reshape(352, 512))
+        image_scale = xi[:, :, :, PACKED:PACKED + 128].reshape(16, 16, 128)[:, 0:8].astype(F32).reshape(128, 128)
+        image_scale = image_scale[:, 0:1] + image_scale[:, 64:65]
+        for b in range(2):
+            gate_up = lows[b].reshape(16, 16, 352)[:, 0:8] + highs[b].reshape(16, 16, 352)[:, 8:16]
+            gate_up = gate_up.reshape(128, 352) * image_scale
+            image_act.append(active(gate_up[:, 0:176], gate_up[:, 176:352]))
 
     def sum_one(d, n):
         if n % 2 == 0:
-            src, device = isend.at[d, :, :, chunk[n]], at.dev(dy=4 - d)
+            src, device = isend.at[d, :, :, half[n]], at.dev(dy=4 - d)
         else:
-            src, device = isend.at[:, d, :, chunk[n]], at.dev(dx=4 - d)
-        return remote(src, ir1.at[d - 1, :, :, chunk[n]], y1_send.at[d, n], y1_recv.at[d, n], device)
+            src, device = isend.at[:, d, :, half[n]], at.dev(dx=4 - d)
+        return remote(src, ir1.at[d - 1, :, :, half[n]], y1_send.at[d, n], y1_recv.at[d, n], device)
 
     def sum_two(d, n):
         device = at.dev(dx=4 - d) if n % 2 == 0 else at.dev(dy=4 - d)
-        return remote(is2.at[d, :, chunk[n]], ir2.at[d - 1, :, chunk[n]], y2_send.at[d, n], y2_recv.at[d, n], device)
+        return remote(is2.at[d, :, half[n]], ir2.at[d - 1, :, half[n]], y2_send.at[d, n], y2_recv.at[d, n], device)
 
     def image_down(n):
-        result = jnp.concatenate(
-            [jnp.dot(image_act, wi[e, 2], preferred_element_type=F32) for e in (2 * n, 2 * n + 1)], axis=1
-        )
-        isend[:, :, :, chunk[n]] = result.astype(BF16).reshape(4, 4, 16, CHUNK)
+        parts = []
+        for e in (2 * n, 2 * n + 1):
+            result = sum(jnp.dot(image_act[b], wi[b, e, 2], preferred_element_type=F32) for b in range(2))
+            parts.append(result.reshape(16, 8, HALF))
+        isend[:, :, :, half[n]] = jnp.concatenate(parts, axis=1).astype(BF16).reshape(4, 4, 16, HALF)
         for d in (1, 3, 2):
             sum_one(d, n).start()
 
     def image_turn(n):
-        total = (isend[0, :, :, chunk[n]] if n % 2 == 0 else isend[:, 0, :, chunk[n]]).astype(F32)
+        total = (isend[0, :, :, half[n]] if n % 2 == 0 else isend[:, 0, :, half[n]]).astype(F32)
         for d in (1, 3, 2):
             sum_one(d, n).wait_recv()
-            total += ir1[d - 1, :, :, chunk[n]].astype(F32)
-        is2[:, :, chunk[n]] = total.astype(BF16)
+            total += ir1[d - 1, :, :, half[n]].astype(F32)
+        is2[:, :, half[n]] = total.astype(BF16)
         for d in (1, 3, 2):
             sum_two(d, n).start()
 
@@ -499,12 +512,7 @@
 
     def combine(n):
         each(1, 16, lambda t: text_back(t, n).wait_recv())
-        image_total = is2[0, :, chunk[n]].astype(F32)
-        for d in (1, 3, 2):
-            sum_two(d, n).wait_recv()
-            image_total += ir2[d - 1, :, chunk[n]].astype(F32)
         total = tn_dot(back_map[...], ys[:, :, chunk[n]].reshape(256, CHUNK))
-        total += tn_dot(image_map[...], image_total.astype(BF16))
         total = total.reshape(8, 16, CHUNK)
         zsend[:, :, chunk[n]] = total.astype(BF16)
         for i in (2, 1, 3):
@@ -530,30 +538,74 @@
         for dz in range(1, 8):
             from_column(dz, n).wait_recv()
             total += zrecv[dz, :, chunk[n]].astype(F32)
-        out_ref[:, chunk[n]] = total.astype(BF16)
+        state[:, chunk[n]] = total
 
         @pl.when(odd)
         def _():
             from_column(0, n).wait_recv()
-            out_ref[:, chunk[n]] = (total + zrecv[0, :, chunk[n]].astype(F32)).astype(BF16)
-
+            state[:, chunk[n]] = total + zrecv[0, :, chunk[n]].astype(F32)
+
+    def spot_swap(n):
+        return remote(
+            spots.at[z, :, chunk[n]], spot_recv.at[:, chunk[n]], s_send.at[n], s_recv.at[n], at.dev(dzl=1, dk=1)
+        )
+
+    def image_out(n):
+        image_total = is2[0, :, half[n]].astype(F32)
+        for d in (1, 3, 2):
+            sum_two(d, n).wait_recv()
+            image_total += ir2[d - 1, :, half[n]].astype(F32)
+        image_total = image_total.astype(BF16)
+        spread = jnp.concatenate([tn_dot(image_map[b], image_total) for b in range(2)], axis=1)
+        spots[:, :, chunk[n]] = spread.astype(BF16).reshape(8, 16, CHUNK)
+
+        @pl.when(odd)
+        def _():
+            spot_swap(n).start()
+
+    def image_end(n):
+        @pl.when(even)
+        def _():
+            out_ref[:, chunk[n]] = (state[:, chunk[n]] + spots[z, :, chunk[n]].astype(F32)).astype(BF16)
+
+        @pl.when(odd)
+        def _():
+            spot_swap(n).wait_recv()
+            out_ref[:, chunk[n]] = (state[:, chunk[n]] + spot_recv[:, chunk[n]].astype(F32)).astype(BF16)
+
+    text_down(0)
+    text_down(1)
+    text_down(2)
+    text_down(3)
+    image_step(3)
+    combine(0)
+    combine(1)
+    image_ready()
     image_down(0)
     image_down(1)
-    text_down(2)
     image_down(2)
+    image_down(3)
+    combine(2)
+    finish(0)
     image_turn(0)
-    text_down(3)
-    image_down(3)
-    for n in range(CHUNKS):
-        if n + 1 < CHUNKS:
-            image_turn(n + 1)
-        combine(n)
-        if n > 0:
-            finish(n - 1)
-    finish(CHUNKS - 1)
+    image_turn(1)
+    combine(3)
+    finish(1)
+    image_turn(2)
+    image_turn(3)
+    image_out(0)
+    finish(2)
+    image_out(1)
+    image_end(0)
+    image_out(2)
+    image_end(1)
+    image_out(3)
+    image_end(2)
+    finish(3)
+    image_end(3)
 
     meta_copy.wait_send()
-    for copy in kv[0] + kv[1] + swap + swaps + sums + image_copies:
+    for copy in kv[0] + kv[1] + swap + swaps + sums:
         copy.wait_send()
     for h in range(2):
         def sent_a(j):
@@ -561,10 +613,11 @@
             back(h, j).wait_send()
 
         each(1, 8, sent_a)
-    for d in (1, 2, 3):
-        image_pass(d).wait_send()
-    for d in (1, 3):
-        image_half(d).wait_send()
+    for dz in range(-3, 5):
+        image_pass(dz).wait_send()
+    for i in range(4):
+        for side in range(2):
+            image_ring(side, i, i).wait_send()
     for n in range(CHUNKS):
         def sent_b(t):
             text_copy(t, n).wait_send()
@@ -585,6 +638,7 @@
         @pl.when(odd)
         def _():
             pair_copy(n).wait_send()
+            spot_swap(n).wait_send()
             for core in range(2):
                 to_owner(0, core, n).wait_send()
 
@@ -618,16 +672,16 @@
             buf(256, WIDTH), buf(16, WIDTH), buf(256, 128),
             buf(2, 4, 16, WIDTH), buf(4, 16, WIDTH), buf(4, 16, WIDTH), buf(3, 16, WIDTH),
             buf(16, WIDTH, dtype=F32), buf(16, WIDE),
-            buf(704, WIDTH), buf(704, WIDTH), buf(704, WIDTH), buf(8, 3, 176, 512),
-            buf(16, 128, dtype=F32), buf(16, 128, dtype=F32), buf(256, 128), buf(256, 128), buf(16, 128),
-            buf(4, 2, 16, WIDE), buf(16, 16, WIDE), buf(16, 16, WIDE), buf(4, 4, 16, WIDE),
+            buf(704, WIDTH), buf(704, WIDTH), buf(704, WIDTH), buf(2, 8, 3, 176, 512),
+            buf(16, 128, dtype=F32), buf(16, 128, dtype=F32), buf(256, 128), buf(256, 128), buf(2, 16, 128),
+            buf(4, 2, 16, WIDE), buf(16, 16, WIDE), buf(16, 16, WIDE), buf(4, 4, 16, PACKED + 128),
             buf(2, 256, 704, dtype=F32),
-            buf(16, 16, WIDTH), buf(16, 16, WIDTH), buf(4, 4, 16, WIDTH), buf(3, 4, 16, WIDTH),
-            buf(4, 16, WIDTH), buf(3, 16, WIDTH), buf(8, 16, WIDTH), buf(8, 16, WIDTH), buf(16, WIDTH, dtype=F32),
+            buf(16, 16, WIDTH), buf(16, 16, WIDTH), buf(4, 4, 16, PACKED), buf(3, 4, 16, PACKED),
+            buf(4, 16, PACKED), buf(3, 16, PACKED), buf(8, 16, WIDTH), buf(8, 16, WIDTH), buf(16, WIDTH, dtype=F32), buf(8, 16, WIDTH), buf(16, WIDTH),
             *pair(2, 2, 4), *pair(2, 8), *pair(2, 8), *pair(CHUNKS), *pair(CHUNKS, 4), dma((11,)),
             *pair(3), dma, dma, *pair(CHUNKS), *pair(2, 2, CHUNKS), *pair(16, CHUNKS),
-            *pair(4, CHUNKS), *pair(4, CHUNKS), *pair(4), *pair(4), *pair(4), *pair(16, CHUNKS),
-            *pair(4, CHUNKS), *pair(4, CHUNKS), dma((4, 2, CHUNKS)), dma((8, CHUNKS)),
+            *pair(4, CHUNKS), *pair(4, CHUNKS), *pair(2, 4), *pair(8), *pair(16, CHUNKS),
+            *pair(4, CHUNKS), *pair(4, CHUNKS), dma((4, 2, CHUNKS)), dma((8, CHUNKS)), *pair(CHUNKS),
         ],
         compiler_params=pltpu.CompilerParams(
             collective_id=1, has_side_effects=True, vmem_limit_bytes=60 << 20

time: 161 us -> 148 us (0.919); the launches traced: 161 us -> 145 us
  Pallas kernels: 159 us -> 144 us
    pallas_call x1, Pallas kernels: 159 us -> 144 us  [body(): pl.pallas_call(layer_kernel, name='layer', out_shape=jax.ShapeDtypeStruct...]
where the time goes in v5:
time: 148 us; the launch traced here: 145 us
  Pallas kernels  144 us (97%)
  local copies, waits for them, and re-layouts  1.57 us (1%)
    pallas_call x1, Pallas kernels, body(): pl.pallas_call(layer_kernel, name='layer', out_shape=jax.ShapeDtypeStruct...  144 us

profile of v5, /device:TPU:1, one launch (start us, length us, event | category | flops | bytes accessed | tf_op | source)
XLA Modules:
  0.0 145.1 jit_solution(7647373282971367541)
XLA Ops:
  0.0 143.6 %layer.1 = bf16[16,4096]{1,0:T(8,128)(2,1)} custom-call(bf16[128,256]{1,0:T(8,128)(2,1)} %q_ref.1, bf16[128,256]{1,0:T(8,128)(2,1)} %k_ref.1, bf16[128,256]{1,0:T(8,128)(2,1)} %v_ref.1, bf16[128,4096]{1,0:T(8,128)(2,1)} %resid_ref.1, s32[1,128]{1,0:T(1,128)} %bitcast.17, s32[6,128]{1,0:T(8,128)} %bitcast.15, bf16[6,128]{1,0:T(8,128)(2,1)} %bitcast.16, ...), custom_call_target="tpu_custom_call" | custom-call | tf_op jit(solution)/shard_map/layer/pallas_call | solution.py:664
  143.6 1.6 %copy.17 = bf16[16,4096]{1,0:T(8,128)(2,1)} copy(bf16[16,4096]{1,0:T(8,128)(2,1)} %layer.1) | data formatting | bytes 262144

commit v6 on v5

--- a/solution.py
+++ b/solution.py
@@ -400,7 +400,7 @@
         for d in (1, 3, 2):
             second_hop(d, n).start()
 
-    for step in range(CHUNKS + 3):
+    for step in range(CHUNKS + 2):
         if step < CHUNKS:
             norm_step(step)
         if 0 <= step - 1 < CHUNKS:
@@ -410,9 +410,9 @@
             if step - 2 == CHUNKS - 1:
                 image_step(1)
             dispatch(step - 2)
-        if 0 <= step - 3 < CHUNKS:
-            forward(step - 3)
-
+
+    for n in range(CHUNKS):
+        forward(n)
     for copy in weights[:2]:
         copy.wait()
     for copy in swap[:2]:
@@ -426,7 +426,7 @@
                 acc[i] = term
             else:
                 acc[i] += term
-        if n == 1:
+        if n == 0:
             image_step(2)
     text_scale = xt[:, :, SCALE:WIDE].reshape(256, 128).astype(F32)
     text_scale = text_scale[:, 0:1] + text_scale[:, 64:65]
@@ -575,9 +575,9 @@
 
     text_down(0)
     text_down(1)
+    image_step(3)
     text_down(2)
     text_down(3)
-    image_step(3)
     combine(0)
     combine(1)
     image_ready()

time: 148 us -> 146 us (0.986); the launches traced: 145 us -> 146 us
  no operation moved by 1% of the time
where the time goes in v6:
time: 146 us
  Pallas kernels  144 us (99%)
  local copies, waits for them, and re-layouts  1.57 us (1%)
    pallas_call x1, Pallas kernels, body(): pl.pallas_call(layer_kernel, name='layer', out_shape=jax.ShapeDtypeStruct...  144 us

profile of v6, /device:TPU:1, one launch (start us, length us, event | category | flops | bytes accessed | tf_op | source)
XLA Modules:
  0.0 145.6 jit_solution(11497776785901152994)
XLA Ops:
  0.0 144.0 %layer.1 = bf16[16,4096]{1,0:T(8,128)(2,1)} custom-call(bf16[128,256]{1,0:T(8,128)(2,1)} %q_ref.1, bf16[128,256]{1,0:T(8,128)(2,1)} %k_ref.1, bf16[128,256]{1,0:T(8,128)(2,1)} %v_ref.1, bf16[128,4096]{1,0:T(8,128)(2,1)} %resid_ref.1, s32[1,128]{1,0:T(1,128)} %bitcast.17, s32[6,128]{1,0:T(8,128)} %bitcast.15, bf16[6,128]{1,0:T(8,128)(2,1)} %bitcast.16, ...), custom_call_target="tpu_custom_call" | custom-call | tf_op jit(solution)/shard_map/layer/pallas_call | solution.py:664
  144.0 1.6 %copy.17 = bf16[16,4096]{1,0:T(8,128)(2,1)} copy(bf16[16,4096]{1,0:T(8,128)(2,1)} %layer.1) | data formatting | bytes 262144
